TPU v7x, 256 devices: a whole 4x4x8 slice. The times are simulated.
256 devices in a mesh: ctx: 64 (over z, x, core), head: 4 (over y).
Axes of the slice: x: 4, y: 4, z: 8, core: 2. Of those that a mesh axis runs over, the one named last changes fastest.
Arguments:
- queries: bfloat16 [65536, 2048], P('ctx', 'head'), may hold values from -6 to 6
- keys: bfloat16 [65536, 2048], P('ctx', 'head'), may hold values from -6 to 6
- values: bfloat16 [65536, 4096], P('ctx', 'head'), may hold values from -6 to 6
- log_gate: bfloat16 [65536, 2048], P('ctx', 'head'), may hold values from -1.7 to 0, as said below
- out_gate: bfloat16 [65536, 4096], P('ctx', 'head'), may hold values from -6 to 6
- segment_ids: int32 [512], replicated, may hold values from 0 to 3, never falling along the last dimension, each value on 1 to 256 neighbouring positions
- final_projector: bfloat16 [4096, 4096], P('head'), may hold values from -0.09375 to 0.09375
Outputs:
- projected: bfloat16 [65536, 4096], P('ctx', 'head')
Inputs may be any that keep to these rules, and one draw needn't show every extreme that they name: `segment_ids`: segment numbers never fall; a segment spans at most 256 blocks. `log_gate`: logarithm of a decay factor.
All inputs are finite; a program needn't handle non-finite values.
Results may differ from a plain program's by a relative error of at most 0.013.
Values may be sent and summed in bfloat16 or wider, within the bound.
A program may use at most 192 MiB of HBM per device.

v0:
```python
import jax
import jax.numpy as jnp
from jax import lax
from jax.sharding import PartitionSpec as P

DK = 128
DV = 256
CH = 128


def prefix(value, axis, join, neutral):
    count, mine = (lax.axis_size(axis), lax.axis_index(axis))
    pieces = jax.tree.map(lambda part: lax.all_gather(part, axis), value)
    running = jax.tree.map(
        lambda part, zero: jnp.full_like(part, 0) + jnp.asarray(zero, part.dtype), value, neutral
    )

    def step(position, running):
        longer = join(running, jax.tree.map(lambda part: part[position], pieces))
        return jax.tree.map(lambda new, old: jnp.where(position < mine, new, old), longer, running)

    return lax.fori_loop(0, count - 1, step, running)


def compose(earlier_map, later_map):
    return (earlier_map[0] * later_map[0], later_map[0][..., None] * earlier_map[1] + later_map[1])


def shards(queries, keys, values, log_gate, out_gate, segment_ids, final_projector):
    tokens_here = queries.shape[0]
    heads_here = queries.shape[1] // DK
    blocks = tokens_here // CH
    row_ids = lax.broadcasted_iota(jnp.int32, (CH, CH), 0)
    col_ids = lax.broadcasted_iota(jnp.int32, (CH, CH), 1)
    causal = col_ids <= row_ids
    rate_rows = log_gate.astype(jnp.float32).reshape(blocks, CH, heads_here * DK)
    running = jnp.einsum(
        "ij,njc->nic", causal.astype(jnp.float32), rate_rows, precision=lax.Precision.HIGHEST
    )
    running = running.reshape(blocks, CH, heads_here, DK)
    final_sum = running[:, -1]
    query_f = queries.astype(jnp.float32).reshape(blocks, CH, heads_here, DK)
    key_f = keys.astype(jnp.float32).reshape(blocks, CH, heads_here, DK)
    decayed_q = query_f * jnp.exp(running) * DK ** (-0.5)
    decayed_k = key_f * jnp.exp(-running)
    kept_k = (key_f * jnp.exp(final_sum[:, None] - running)).astype(jnp.bfloat16)
    payload_tiles = values.reshape(blocks, CH, heads_here, DV)
    scores = jnp.einsum("nihc,njhc->nhij", decayed_q, decayed_k, precision=lax.Precision.HIGHEST)
    probs_bf = jnp.where(causal, scores, 0.0).astype(jnp.bfloat16)
    within_block_output = jnp.einsum(
        "nhij,njhd->nihd", probs_bf, payload_tiles, preferred_element_type=jnp.float32
    )
    local_terms = jnp.einsum(
        "njhc,njhd->nhcd", kept_k, payload_tiles, preferred_element_type=jnp.float32
    )
    decays = jnp.exp(final_sum)
    first_block = lax.axis_index("ctx") * blocks
    padded = jnp.concatenate([segment_ids[:1] - 1, segment_ids])
    current = lax.dynamic_slice_in_dim(padded, first_block + 1, blocks)
    before = lax.dynamic_slice_in_dim(padded, first_block, blocks)
    keep_flags = (current == before).astype(jnp.float32)
    factor = decays * keep_flags[:, None, None]
    identity = (
        jnp.ones((heads_here, DK), jnp.float32),
        jnp.zeros((heads_here, DK, DV), jnp.float32),
    )

    def fold_step(running_map, single_entry):
        return (compose(running_map, single_entry), None)

    summary, _ = lax.scan(fold_step, identity, (factor, local_terms))
    _, incoming = prefix(summary, "ctx", compose, identity)

    def advance(pair_now, single_entry):
        state_now, weight_now = pair_now
        decay_one, keep_one, local_one = single_entry
        start_state = keep_one * state_now
        start_weight = keep_one * weight_now
        return (
            (decay_one[..., None] * start_state + local_one, decay_one * start_weight),
            (start_state, start_weight),
        )

    identity_coefficient = jnp.ones((heads_here, DK), jnp.float32)
    _, (segment_start_index, _) = lax.scan(
        advance, (incoming, identity_coefficient), (decays, keep_flags, local_terms)
    )
    carried = jnp.einsum(
        "nihc,nhcd->nihd", decayed_q, segment_start_index, precision=lax.Precision.HIGHEST
    )
    mixed_out = (carried + within_block_output).reshape(tokens_here, heads_here, DV)
    scaled = mixed_out * lax.rsqrt(jnp.mean(mixed_out * mixed_out, axis=-1, keepdims=True) + 1e-05)
    gate_vals = out_gate.astype(jnp.float32).reshape(tokens_here, heads_here, DV)
    latent_width = (
        (scaled * jax.nn.silu(gate_vals)).astype(jnp.bfloat16).reshape(tokens_here, heads_here * DV)
    )
    unfinished_summands = jnp.dot(latent_width, final_projector, preferred_element_type=jnp.float32)
    projected = lax.psum_scatter(
        unfinished_summands.astype(jnp.bfloat16), "head", scatter_dimension=1, tiled=True
    )
    return projected


def solution(mesh):
    return jax.shard_map(
        shards,
        mesh=mesh,
        in_specs=(
            P("ctx", "head"),
            P("ctx", "head"),
            P("ctx", "head"),
            P("ctx", "head"),
            P("ctx", "head"),
            P(),
            P("head", None),
        ),
        out_specs=P("ctx", "head"),
        check_vma=False,
    )
```

profile of v0, /device:TPU:1, one launch (start us, length us, event | category | flops | bytes accessed | tf_op | source)
XLA Modules:
  0.0 414.6 jit_solution(3628211672386707952)
XLA Ops:
  8.2 1.7 reshape.52
  9.9 2.9 copy.29
  15.7 2.7 reshape.60
  18.4 2.9 copy.30
  21.3 4.5 %reshape.55 = bf16[8,128,4,256]{3,2,1,0:T(4,128)(2,1)} reshape(bf16[1024,1024]{1,0:T(8,128)(2,1)} %param.15) | data formatting | bytes 4194304 | tf_op jit(solution)/shard_map/reshape | solution.py:47
  25.8 5.7 %fusion.15 = f32[8,4,128,256]{3,2,1,0:T(8,128)} fusion(bf16[8,128,4,256]{3,2,1,0:T(4,128)(2,1)} %reshape.55, f32[8,128,4,128]{1,3,2,0:T(8,128)} %copy.30, f32[8,128,4,128]{1,3,2,0:T(8,128)} %copy.29, f32[8,4,128]{2,1,0:T(4,128)S(1)} %slice_bitcast_fusion), kind=kOutput, calls=%fused_computation.33 | convolution fusion | flops 270008320 | bytes 10502144 | tf_op jit(solution)/shard_map/njhc,njhd->nhcd/dot_general | solution.py:53
  31.5 10.0 %while.40 = (s32[]{:T(128)}, f32[4,128]{1,0:T(4,128)S(1)}, f32[4,128,256]{2,1,0:T(8,128)S(1)}, f32[8,4,128]{2,1,0:T(4,128)S(1)}, f32[8,4,128,256]{3,2,1,0:T(8,128)}, /*index=5*/s32[]{:T(128)}, s32[]{:T(128)}) while((s32[]{:T(128)}, f32[4,128]{1,0:T(4,128)S(1)}, f32[4,128,256]{2,1,0:T(8,128)S(1)}, f32[8,4,128]{2,1,0:T(4,128)S(1)}, ...), condition=%wide.region_1.2_spmd.clone, body=%wide.region_0.1_spmd.clone.sunk | while | flops 394243 | bytes 1583200 | solution.py:71
  42.5 2.7 reshape.62
  45.2 3.9 copy.40
  49.1 54.1 %all-gather.2 = f32[64,4,128]{2,1,0:T(4,128)S(1)} all-gather(f32[1,4,128]{2,1,0:T(4,128)S(1)} %bitcast.101), channel_id=2, replica_groups=mesh['ctx'=64,'head'=4] {'ctx'}, dimensions={0}, use_global_device_ids=true | all-gather | bytes 133120 | tf_op jit(solution)/shard_map/all_gather | solution.py:13
  103.2 7.9 %select_convert_fusion = bf16[8,4,128,128]{3,2,1,0:T(8,128)(2,1)} fusion(f32[8,128,4,128]{3,2,1,0:T(4,128)} %reshape.60, f32[8,128,4,128]{3,2,1,0:T(4,128)} %reshape.62, pred[128,128]{1,0:T(8,128)(4,1)S(1)} %iota_compare_fusion, f32[128,8,512]{2,0,1:T(8,128)S(1)} %fusion.25), kind=kOutput, calls=%fused_computation.29 | convolution fusion | flops 808452096 | bytes 7356416 | tf_op jit(solution)/shard_map/nihc,njhc->nhij/dot_general | solution.py:48
  111.1 77.9 %all-gather.5.cloned.1.call-done = f32[256,128,256]{2,1,0:T(8,128)} async-done(((f32[4,128,256]{2,1,0:T(8,128)}), f32[256,128,256]{2,1,0:T(8,128)}) %all-gather.5.cloned.1.call-update) | async-done | bytes 33554448 | tf_op jit(solution)/shard_map/all_gather | solution.py:13
  189.0 80.9 %while.41 = (s32[]{:T(128)}, f32[4,128,256]{2,1,0:T(8,128)S(1)}, s32[]{:T(128)}, f32[64,4,128]{2,1,0:T(4,128)S(1)}, f32[64,4,128,256]{3,2,1,0:T(8,128)}, /*index=5*/s32[]{:T(128)}, s32[]{:T(128)}) while((s32[]{:T(128)}, f32[4,128,256]{2,1,0:T(8,128)S(1)}, s32[]{:T(128)}, f32[64,4,128]{2,1,0:T(4,128)S(1)}, ...), condition=%wide.region_3.4_spmd.clone, body=%wide.region_2.3_spmd.clone.sunk | while | flops 524292 | bytes 1579113 | solution.py:22
  269.9 31.8 %while.39 = (s32[]{:T(128)}, f32[4,128,256]{2,1,0:T(8,128)S(1)}, f32[8,4,128,256]{3,2,1,0:T(8,128)}, f32[8,4,128]{2,1,0:T(4,128)S(1)}, f32[8]{0:T(128)S(1)}, /*index=5*/f32[8,4,128,256]{3,2,1,0:T(8,128)}, s32[]{:T(128)}) while((s32[]{:T(128)}, f32[4,128,256]{2,1,0:T(8,128)S(1)}, f32[8,4,128,256]{3,2,1,0:T(8,128)}, f32[8,4,128]{2,1,0:T(4,128)S(1)}, ...), condition=%wide.region_5.6_spmd, body=%wide.region_4.5_spmd.sunk | while | flops 524290 | bytes 2628709 | solution.py:85
  272.0 1.9 bitcast_add_fusion.6
  274.5 1.5 bitcast_dynamic-update-slice_fusion.2
  276.0 1.9 bitcast_add_fusion.6
  280.0 1.9 bitcast_add_fusion.6
  282.5 1.5 bitcast_dynamic-update-slice_fusion.2
  283.9 1.9 bitcast_add_fusion.6
  286.4 1.5 bitcast_dynamic-update-slice_fusion.2
  287.9 1.9 bitcast_add_fusion.6
  291.9 1.9 bitcast_add_fusion.6
  294.4 1.5 bitcast_dynamic-update-slice_fusion.2
  295.9 1.9 bitcast_add_fusion.6
  298.4 1.5 bitcast_dynamic-update-slice_fusion.2
  299.9 1.9 bitcast_add_fusion.6
  301.8 9.5 %fusion.20 = f32[8,4,256,128]{3,2,1,0:T(8,128)S(1)} fusion(f32[8,4,128,256]{3,2,1,0:T(8,128)} %get-tuple-element.162, f32[8,128,4,128]{3,2,1,0:T(4,128)} %reshape.62, f32[128,8,512]{2,0,1:T(8,128)S(1)} %fusion.25), kind=kOutput, calls=%fused_computation.35 | convolution fusion | flops 1611661312 | bytes 12582912 | tf_op jit(solution)/shard_map/nihc,nhcd->nihd/dot_general | solution.py:88
  312.3 2.4 copy.39
  314.8 1.6 fusion.5
  316.4 11.4 %convolution_convert_fusion = bf16[1024,4096]{1,0:T(8,128)(2,1)} fusion(bf16[1024,1024]{0,1:T(8,128)(2,1)S(1)} %fusion.5, bf16[1024,4096]{1,0:T(8,128)(2,1)S(1)} %bitcast.103), kind=kOutput, calls=%fused_computation.10 | convolution fusion | flops 8594128896 | bytes 18874368 | tf_op jit(solution)/shard_map/dot_general | solution.py:97
  327.8 79.9 %reduce-scatter.2.cloned.1.call-done = bf16[1024,1024]{1,0:T(8,128)(2,1)} async-done(((bf16[1024,4096]{1,0:T(8,128)(2,1)}), bf16[1024,1024]{1,0:T(8,128)(2,1)}) %reduce-scatter.2.cloned.1.call-update) | async-done | bytes 2097168 | tf_op jit(solution)/shard_map/reduce_scatter | solution.py:98
  (197 shorter events, 103.6 us)
Async XLA Ops:
  6.5 1.2 copy-start
  6.5 182.5 %all-gather.5.cloned.1.call-start = ((), (), s32[]{:S(2)}) async-start(), calls=%async_computation.2 | async-start | bytes 34078720 | tf_op jit(solution)/shard_map/all_gather | solution.py:13
  9.9 3.6 copy-start.6
  41.5 0.9 copy-start.2
  42.4 365.3 %reduce-scatter.2.cloned.1.call-start = ((), (), s32[]{:S(2)}) async-start(), calls=%async_computation.1 | async-start | bytes 10485760 | tf_op jit(solution)/shard_map/reduce_scatter | solution.py:98
  301.7 9.5 %copy-start.3 = (bf16[8,128,4,256]{3,2,1,0:T(4,128)(2,1)S(1)}, bf16[8,128,4,256]{3,2,1,0:T(4,128)(2,1)}, u32[]{:S(2)}) copy-start(bf16[8,128,4,256]{3,2,1,0:T(4,128)(2,1)} %reshape.55) | copy-start | bytes 6291460
  301.8 9.5 %copy-start.5 = (bf16[8,4,128,128]{3,2,1,0:T(8,128)(2,1)S(1)}, bf16[8,4,128,128]{3,2,1,0:T(8,128)(2,1)}, u32[]{:S(2)}) copy-start(bf16[8,4,128,128]{3,2,1,0:T(8,128)(2,1)} %select_convert_fusion) | copy-start | bytes 3145732
  311.3 5.1 %slice-start = ((s8[8388608]{0:T(1024)(128)(4,1)}), s8[4194304]{0:T(1024)(128)(4,1)S(1)}, s32[]{:S(2)}) async-start(s8[8388608]{0:T(1024)(128)(4,1)} %bitcast.102), calls=%async_computation.3 | async-start | bytes 8388608
  312.3 2.5 copy-start.4
  312.3 4.1 slice-start.1
  327.8 79.9 %copy-start.1 = (bf16[1024,512]{1,0:T(8,128)(2,1)S(1)}, bf16[1024,512]{1,0:T(8,128)(2,1)}, u32[]{:S(2)}) copy-start(bf16[1024,512]{1,0:T(8,128)(2,1)} %param.16) | copy-start | bytes 3145732
Sparse Core Ops, SparseCore 0:
  42.5 146.4 all-gather.4
  328.0 79.7 reduce-scatter.1
where the time goes:
time: 419 us; the launch traced here: 415 us
  waiting for transfers between devices  158 us (38%)
  other arithmetic  117 us (28%)
  blocking collectives  54.1 us (13%)
  matrix products  36 us (9%)
  local copies, waits for them, and re-layouts  32.6 us (8%)
  between operations  14.2 us (3%)
    reduce_scatter x1, waiting for transfers between devices, shards(): lax.psum_scatter(unfinished_summands.astype(jnp.bfloat16), 'head', scatte...  79.9 us
    select_n x63, other arithmetic, step(): jnp.where(position < mine, new, old)  78.1 us
    all_gather x1, waiting for transfers between devices, prefix(): pieces = jax.tree.map(lambda part: lax.all_gather(part, axis), value)  77.9 us
    all_gather x1, blocking collectives, prefix(): pieces = jax.tree.map(lambda part: lax.all_gather(part, axis), value)  54.1 us
    add x8, other arithmetic, advance(): decay_one[..., None] * start_state + local_one  14.8 us
    dynamic_update_slice x8, other arithmetic, shards(): lax.scan(advance, (incoming, identity_coefficient), (decays, keep_flags,...  11.9 us
    dot_general x1, matrix products, shards(): jnp.dot(latent_width, final_projector, preferred_element_type=jnp.float32)  11.4 us
    add x8, other arithmetic, compose(): later_map[0][..., None] * earlier_map[1] + later_map[1]  9.7 us
  transfers between devices with their start and end apart: 2, of which 2 were waited for; matrix products, arithmetic and copies ran while one was open for 4% of the time, Pallas kernels for 0%

commit v1 on v0

v1 whole, which is shorter than its diff:
```python
import jax
import jax.numpy as jnp
from jax import lax
from jax.experimental import pallas as pl
from jax.experimental.pallas import tpu as pltpu
from jax.sharding import PartitionSpec as P

DK = 128
DV = 256
CH = 128
F32 = jnp.float32
BF16 = jnp.bfloat16
MESH = pl.DeviceIdType.MESH

NX = 4
NZ = 8
REACH = 4


def dot(a, b, dims):
    return lax.dot_general(a, b, (dims, ((), ())), preferred_element_type=F32)


def local_kernel(keep, q, k, v, g, mixed, reach_q, state_out, decay_out, state, weight):
    b = pl.program_id(0)
    heads = q.shape[1] // DK

    @pl.when(b == 0)
    def _():
        state[...] = jnp.zeros_like(state)
        weight[...] = jnp.ones_like(weight)

    keep_b = keep[b]
    rows = lax.broadcasted_iota(jnp.int32, (CH, CH), 0)
    cols = lax.broadcasted_iota(jnp.int32, (CH, CH), 1)
    causal = cols <= rows
    cum = dot(causal.astype(F32).astype(BF16), g[...], ((1,), (0,)))
    last = cum[CH - 1 : CH, :]
    qf = q[...].astype(F32)
    kf = k[...].astype(F32)
    dq = qf * jnp.exp(cum) * DK ** (-0.5)
    dk = (kf * jnp.exp(-cum)).astype(BF16)
    kept = (kf * jnp.exp(last - cum)).astype(BF16)
    decay = jnp.exp(last)
    w = weight[...] * keep_b
    reach_q[...] = (dq * w).astype(BF16)
    weight[...] = w * decay
    dq = dq.astype(BF16)
    for h in range(heads):
        kc = slice(h * DK, (h + 1) * DK)
        vc = slice(h * DV, (h + 1) * DV)
        scores = dot(dq[:, kc], dk[:, kc], ((1,), (1,)))
        probs = jnp.where(causal, scores, 0.0).astype(BF16)
        start = state[:, kc] * keep_b
        out = dot(probs, v[:, vc], ((1,), (0,)))
        out += dot(dq[:, kc], start.astype(BF16), ((1,), (1,)))
        mixed[:, vc] = out.astype(BF16)
        local = dot(v[:, vc], kept[:, kc], ((0,), (0,)))
        state[:, kc] = start * decay[:, kc] + local

    @pl.when(b == pl.num_programs(0) - 1)
    def _():
        state_out[...] = state[...].astype(BF16)
        decay_out[...] = weight[...]


def exchange_kernel(
    state, decay, mixed_h, reach_h, gate_h, proj_h, out_h,
    mixed, reach, gate, wo, wp, hid, hid_peer, send, recv, res, own,
    p1, a1, xs, acc, t_out, a_out, t_in, a_in, plane, p3, e_in,
    s_p1, r_p1, s_a1, r_a1, s_p2, r_p2, s_a2, r_a2, s_p3, r_p3,
    s_w1, r_w1, s_wx, r_wx, s_wf, r_wf, s_ws, r_ws,
    s_hid, r_hid, s_rs, r_rs, s_load, s_out,
):
    ctx = lax.axis_index("ctx")
    y = lax.axis_index("head")
    z = ctx // (2 * NX)
    me = ctx % (2 * NX)
    x = me // 2
    core = me % 2
    base = z * (2 * NX)
    pair = y + 1 - 2 * (y % 2)
    over = 3 - y
    xr = (x + 1) % NX
    xl = (x + NX - 1) % NX
    xo = (x + 2) % NX
    tokens = hid.shape[0]
    chunks = tokens // CH
    width = wo.shape[2]
    depth = wo.shape[1]
    slab = depth // (2 * NX)
    part = p1.shape[1]

    def rdma(src, dst, ssem, rsem, c, h):
        return pltpu.make_async_remote_copy(
            src_ref=src, dst_ref=dst, send_sem=ssem, recv_sem=rsem,
            device_id={"ctx": c, "head": h}, device_id_type=MESH,
        )

    def arrived(dst, ssem, rsem):
        rdma(dst, dst, ssem, rsem, ctx, pair).wait_recv()

    def left(src, ssem, rsem):
        rdma(src, src, ssem, rsem, ctx, pair).wait_send()

    mine_cols = pl.ds(pl.multiple_of(y * width, width), width)
    over_cols = pl.ds(pl.multiple_of(over * width, width), width)
    loads = [
        pltpu.make_async_copy(mixed_h, mixed, s_load.at[0]),
        pltpu.make_async_copy(reach_h, reach, s_load.at[1]),
        pltpu.make_async_copy(gate_h, gate, s_load.at[2]),
        pltpu.make_async_copy(proj_h.at[:, over_cols], wo.at[1], s_load.at[3]),
        pltpu.make_async_copy(proj_h.at[:, mine_cols], wo.at[0], s_load.at[4]),
    ]
    for load in loads:
        load.start()

    barrier = pltpu.get_barrier_semaphore()

    def greet(c, h):
        pl.semaphore_signal(barrier, inc=1, device_id={"ctx": c, "head": h}, device_id_type=MESH)

    greet(ctx, pair)
    greet(ctx, over)
    for step in range(1, 2 * NX):
        greet(base + (me + step) % (2 * NX), y)
    for far in range(1, REACH + 1):

        @pl.when(z + far < NZ)
        def _():
            greet(ctx + far * 2 * NX, y)

        @pl.when(z - far >= 0)
        def _():
            greet(ctx - far * 2 * NX, y)

    ahead = jnp.minimum(NZ - 1 - z, REACH)
    behind = jnp.minimum(z, REACH)
    pl.semaphore_wait(barrier, 2 * NX + 1 + ahead + behind)

    def rows_of(i):
        return pl.ds(pl.multiple_of(i * part, part), part)

    for step in range(1, 2 * NX):
        i = (me + step) % (2 * NX)
        rdma(decay, a1.at[me], s_a1.at[i], r_a1.at[me], base + i, y).start()
        rdma(state.at[rows_of(i), :], p1.at[me], s_p1.at[i], r_p1.at[me], base + i, y).start()
    p1[me] = state[rows_of(me), :]
    a1[me] = decay[...]

    def slab_of(xx, cc):
        return pl.ds(pl.multiple_of((xx * 2 + cc) * slab, slab), slab)

    def half_of(xx, cc, half):
        return pl.ds(pl.multiple_of((xx * 2 + cc) * slab + half * (slab // 2), slab // 2), slab // 2)

    pair_cols = (
        pl.ds(pl.multiple_of(pair * width, width), width),
        pl.ds(pl.multiple_of((3 - pair) * width, width), width),
    )
    here = slab_of(x, core)
    at_r = base + xr * 2 + core
    at_l = base + xl * 2 + core
    sib = base + x * 2 + 1 - core

    def w1(j):
        return rdma(proj_h.at[here, pair_cols[j]], wp.at[j, here], s_w1.at[j], r_w1.at[j], ctx, pair)

    def along(j, rows, s, r, item, to):
        return rdma(wp.at[j, rows], wp.at[j, rows], s.at[j, item], r.at[j, item], to, y)

    def wait_in(j, rows, s, r, item):
        arrived(wp.at[j, rows], s.at[j, item], r.at[j, item])

    def relays(cc):
        return (
            slab_of(x, cc), slab_of(xl, cc), slab_of(xr, cc), half_of(xo, cc, 0), half_of(xo, cc, 1),
        )

    def stage_a(j):
        arrived(wp.at[j, here], s_w1.at[j], r_w1.at[j])
        along(j, here, s_wx, r_wx, 0, at_r).start()
        along(j, here, s_wx, r_wx, 1, at_l).start()
        along(j, here, s_ws, r_ws, 0, sib).start()

    def stage_b(j):
        wait_in(j, slab_of(xl, core), s_wx, r_wx, 0)
        along(j, half_of(xl, core, 0), s_wf, r_wf, 0, at_r).start()
        along(j, slab_of(xl, core), s_ws, r_ws, 1, sib).start()
        wait_in(j, slab_of(xr, core), s_wx, r_wx, 1)
        along(j, half_of(xr, core, 1), s_wf, r_wf, 1, at_l).start()
        along(j, slab_of(xr, core), s_ws, r_ws, 2, sib).start()

    def stage_c(j):
        wait_in(j, half_of(xo, core, 0), s_wf, r_wf, 0)
        along(j, half_of(xo, core, 0), s_ws, r_ws, 3, sib).start()
        wait_in(j, half_of(xo, core, 1), s_wf, r_wf, 1)
        along(j, half_of(xo, core, 1), s_ws, r_ws, 4, sib).start()

    def stage_d(j):
        for item, rows in enumerate(relays(1 - core)):
            wait_in(j, rows, s_ws, r_ws, item)

    def weights_left(j):
        left(wp.at[j, here], s_w1.at[j], r_w1.at[j])
        for item in range(2):
            left(wp.at[j, here], s_wx.at[j, item], r_wx.at[j, item])
            left(wp.at[j, half_of(x, core, 0)], s_wf.at[j, item], r_wf.at[j, item])
        for item, rows in enumerate(relays(core)):
            left(wp.at[j, rows], s_ws.at[j, item], r_ws.at[j, item])

    w1(1).start()
    w1(0).start()

    for step in range(1, 2 * NX):
        i = (me + step) % (2 * NX)
        arrived(a1.at[i], s_a1.at[i], r_a1.at[i])
        arrived(p1.at[i], s_p1.at[i], r_p1.at[i])

    run = jnp.zeros((part, p1.shape[2]), F32)
    scale = jnp.ones((1, p1.shape[2]), F32)
    for i in range(2 * NX):
        xs[i] = run
        acc[i] = scale
        run = run * a1[i] + p1[i].astype(F32)
        scale = scale * a1[i]
    t_out[...] = run.astype(BF16)
    a_out[...] = scale

    for far in range(1, REACH + 1):

        @pl.when(z + far < NZ)
        def _():
            to = ctx + far * 2 * NX
            rdma(a_out, a_in.at[far - 1], s_a2.at[far - 1], r_a2.at[far - 1], to, y).start()
            rdma(t_out, t_in.at[far - 1], s_p2.at[far - 1], r_p2.at[far - 1], to, y).start()

    stage_a(1)

    plane[...] = jnp.zeros_like(plane)
    for far in range(REACH, 0, -1):

        @pl.when(z - far >= 0)
        def _():
            arrived(a_in.at[far - 1], s_a2.at[far - 1], r_a2.at[far - 1])
            arrived(t_in.at[far - 1], s_p2.at[far - 1], r_p2.at[far - 1])
            plane[...] = plane[...] * a_in[far - 1] + t_in[far - 1].astype(F32)

    for i in range(2 * NX):
        p3[i] = (xs[i] + acc[i] * plane[...]).astype(BF16)
    for step in range(1, 2 * NX):
        i = (me + step) % (2 * NX)
        rdma(p3.at[i], e_in.at[rows_of(me), :], s_p3.at[i], r_p3.at[me], base + i, y).start()
    e_in[rows_of(me), :] = p3[me]

    for load in loads[:3]:
        load.wait()
    stage_b(1)

    for step in range(1, 2 * NX):
        i = (me + step) % (2 * NX)
        arrived(e_in.at[rows_of(i), :], s_p3.at[i], r_p3.at[i])

    heads = reach.shape[1] // DK

    def chunk_rows(c):
        return pl.ds(pl.multiple_of(c * CH, CH), CH)

    def hidden_step(c, carry):
        rows = chunk_rows(c)
        for h in range(heads):
            kc = slice(h * DK, (h + 1) * DK)
            vc = slice(h * DV, (h + 1) * DV)
            full = mixed[rows, vc].astype(F32)
            full += dot(reach[rows, kc], e_in[:, kc], ((1,), (1,)))
            mean = jnp.mean(full * full, axis=-1, keepdims=True)
            val = gate[rows, vc].astype(F32)
            silu = val / (1.0 + jnp.exp(-val))
            hid[rows, vc] = (full * lax.rsqrt(mean + 1e-5) * silu).astype(BF16)
        rdma(hid.at[rows, :], hid_peer.at[rows, :], s_hid.at[c], r_hid.at[c], ctx, pair).start()
        return carry

    lax.fori_loop(0, chunks, hidden_step, 0)

    stage_c(1)
    stage_a(0)
    for load in loads[3:]:
        load.wait()
    stage_d(1)

    tile = 512

    def product(rows, j, n):
        cols = pl.ds(pl.multiple_of(n * tile, tile), tile)
        total = dot(hid[rows, :], wo[j, :, cols], ((1,), (0,)))
        return total + dot(hid_peer[rows, :], wp[j, :, cols], ((1,), (0,))), cols

    lag = 2

    def main_step(c, carry):
        @pl.when(c < chunks)
        def _():
            rows = chunk_rows(c)
            arrived(hid_peer.at[rows, :], s_hid.at[c], r_hid.at[c])

            def column(n, carry):
                total, cols = product(rows, 1, n)
                send[rows, cols] = total.astype(BF16)
                return carry

            lax.fori_loop(0, width // tile, column, 0)
            rdma(send.at[rows, :], recv.at[rows, :], s_rs.at[c], r_rs.at[c], ctx, over).start()

        @pl.when(c == 0)
        def _():
            stage_b(0)

        @pl.when(c == 1)
        def _():
            stage_c(0)

        @pl.when(c == lag)
        def _():
            stage_d(0)

        @pl.when(c >= lag)
        def _():
            d = c - lag
            rows = chunk_rows(d)

            def column(n, carry):
                total, cols = product(rows, 0, n)
                own[:, cols] = total
                return carry

            lax.fori_loop(0, width // tile, column, 0)
            arrived(recv.at[rows, :], s_rs.at[d], r_rs.at[d])
            res[rows, :] = (own[...] + recv[rows, :].astype(F32)).astype(BF16)
            pltpu.make_async_copy(res.at[rows, :], out_h.at[rows, :], s_out.at[d]).start()

        return carry

    lax.fori_loop(0, chunks + lag, main_step, 0)

    for step in range(1, 2 * NX):
        i = (me + step) % (2 * NX)
        left(decay, s_a1.at[i], r_a1.at[i])
        left(p1.at[i], s_p1.at[i], r_p1.at[i])
        left(p3.at[i], s_p3.at[i], r_p3.at[i])
    for far in range(1, REACH + 1):

        @pl.when(z + far < NZ)
        def _():
            left(a_out, s_a2.at[far - 1], r_a2.at[far - 1])
            left(t_out, s_p2.at[far - 1], r_p2.at[far - 1])

    weights_left(1)
    weights_left(0)

    def finish(c, carry):
        rows = chunk_rows(c)
        left(hid.at[rows, :], s_hid.at[c], r_hid.at[c])
        left(send.at[rows, :], s_rs.at[c], r_rs.at[c])
        pltpu.make_async_copy(res.at[rows, :], out_h.at[rows, :], s_out.at[c]).wait()
        return carry

    lax.fori_loop(0, chunks, finish, 0)


def shards(queries, keys, values, log_gate, out_gate, segment_ids, final_projector):
    tokens = queries.shape[0]
    keys_wide = queries.shape[1]
    vals_wide = values.shape[1]
    blocks = tokens // CH
    depth, full = final_projector.shape
    width = full // 4
    slots = 2 * NX
    part = DV // slots
    chunks = tokens // CH

    first_block = lax.axis_index("ctx") * blocks
    padded = jnp.concatenate([segment_ids[:1] - 1, segment_ids])
    current = lax.dynamic_slice_in_dim(padded, first_block + 1, blocks)
    before = lax.dynamic_slice_in_dim(padded, first_block, blocks)
    keep = (current == before).astype(F32)

    def by_block(wide):
        return pl.BlockSpec((CH, wide), lambda b: (b, 0))

    whole = lambda b: (0, 0)
    mixed, reach, state, decay = pl.pallas_call(
        local_kernel,
        grid=(blocks,),
        in_specs=[
            pl.BlockSpec(memory_space=pltpu.SMEM),
            by_block(keys_wide),
            by_block(keys_wide),
            by_block(vals_wide),
            by_block(keys_wide),
        ],
        out_specs=[
            by_block(vals_wide),
            by_block(keys_wide),
            pl.BlockSpec((DV, keys_wide), whole),
            pl.BlockSpec((1, keys_wide), whole),
        ],
        out_shape=[
            jax.ShapeDtypeStruct((tokens, vals_wide), BF16),
            jax.ShapeDtypeStruct((tokens, keys_wide), BF16),
            jax.ShapeDtypeStruct((DV, keys_wide), BF16),
            jax.ShapeDtypeStruct((1, keys_wide), F32),
        ],
        scratch_shapes=[pltpu.VMEM((DV, keys_wide), F32), pltpu.VMEM((1, keys_wide), F32)],
        compiler_params=pltpu.CompilerParams(vmem_limit_bytes=32 * 2**20),
    )(keep, queries, keys, values, log_gate)

    vm = pltpu.VMEM
    dma = pltpu.SemaphoreType.DMA
    return pl.pallas_call(
        exchange_kernel,
        in_specs=[pl.BlockSpec(memory_space=pltpu.VMEM)] * 2 + [pl.BlockSpec(memory_space=pl.ANY)] * 4,
        out_specs=pl.BlockSpec(memory_space=pl.ANY),
        out_shape=jax.ShapeDtypeStruct((tokens, width), BF16),
        scratch_shapes=[
            vm((tokens, vals_wide), BF16),
            vm((tokens, keys_wide), BF16),
            vm((tokens, vals_wide), BF16),
            vm((2, depth, width), BF16),
            vm((2, depth, width), BF16),
            vm((tokens, vals_wide), BF16),
            vm((tokens, vals_wide), BF16),
            vm((tokens, width), BF16),
            vm((tokens, width), BF16),
            vm((tokens, width), BF16),
            vm((CH, width), F32),
            vm((slots, part, keys_wide), BF16),
            vm((slots, 1, keys_wide), F32),
            vm((slots, part, keys_wide), F32),
            vm((slots, 1, keys_wide), F32),
            vm((part, keys_wide), BF16),
            vm((1, keys_wide), F32),
            vm((REACH, part, keys_wide), BF16),
            vm((REACH, 1, keys_wide), F32),
            vm((part, keys_wide), F32),
            vm((slots, part, keys_wide), BF16),
            vm((DV, keys_wide), BF16),
            dma((slots,)), dma((slots,)),
            dma((slots,)), dma((slots,)),
            dma((REACH,)), dma((REACH,)),
            dma((REACH,)), dma((REACH,)),
            dma((slots,)), dma((slots,)),
            dma((2,)), dma((2,)),
            dma((2, 2)), dma((2, 2)),
            dma((2, 2)), dma((2, 2)),
            dma((2, 5)), dma((2, 5)),
            dma((chunks,)), dma((chunks,)),
            dma((chunks,)), dma((chunks,)),
            dma((5,)),
            dma((chunks,)),
        ],
        compiler_params=pltpu.CompilerParams(
            collective_id=0, has_side_effects=True, vmem_limit_bytes=48 * 2**20
        ),
    )(state, decay, mixed, reach, out_gate, final_projector)


def solution(mesh):
    return jax.shard_map(
        shards,
        mesh=mesh,
        in_specs=(
            P("ctx", "head"),
            P("ctx", "head"),
            P("ctx", "head"),
            P("ctx", "head"),
            P("ctx", "head"),
            P(),
            P("head", None),
        ),
        out_specs=P("ctx", "head"),
        check_vma=False,
    )
```

time: 419 us -> 103 us (0.25); the launches traced: 415 us -> 103 us
  waiting for transfers between devices: 158 us -> 0 us
  other arithmetic: 117 us -> 0.84 us
  Pallas kernels: 0 us -> 93.5 us
  blocking collectives: 54.1 us -> 0 us
  matrix products: 36 us -> 0 us
  local copies, waits for them, and re-layouts: 32.6 us -> 7.78 us
  between operations: 14.2 us -> 0.67 us
    pallas_call x0 -> x2, Pallas kernels: none -> 93.5 us  [the longest x1 86.4 us: shards(): pl.pallas_call(exchange_kernel, in_specs=[pl.BlockSpec(memory_space=pltpu...]
    reduce_scatter x1 -> x0, waiting for transfers between devices: 79.9 us -> none  [shards(): lax.psum_scatter(unfinished_summands.astype(jnp.bfloat16), 'head', scatte...]
    select_n x63 -> x0, other arithmetic: 78.1 us -> none  [step(): jnp.where(position < mine, new, old)]
    all_gather x1 -> x0, waiting for transfers between devices: 77.9 us -> none  [prefix(): pieces = jax.tree.map(lambda part: lax.all_gather(part, axis), value)]
    all_gather x1 -> x0, blocking collectives: 54.1 us -> none  [prefix(): pieces = jax.tree.map(lambda part: lax.all_gather(part, axis), value)]
    dot_general x6 -> x0, matrix products: 36 us -> none  [the longest x1 11.4 us: shards(): jnp.dot(latent_width, final_projector, preferred_element_type=jnp.float32)]
    add x16 -> x0, other arithmetic: 24.5 us -> none  [the longest x8 14.8 us: advance(): decay_one[..., None] * start_state + local_one]
    reshape x6 -> x0, local copies, waits for them, and re-layouts: 17.4 us -> none  [the longest x2 5.6 us: shards(): key_f = keys.astype(jnp.float32).reshape(blocks, CH, heads_here, DK)]
  transfers between devices with their start and end apart: 2 -> 0, of which waited for: 2 -> 0; matrix products, arithmetic and copies ran while one was open for 4% -> 0% of each run, Pallas kernels for 0% -> 0%
where the time goes in v1:
time: 103 us
  Pallas kernels  93.5 us (91%)
  local copies, waits for them, and re-layouts  7.78 us (8%)
    pallas_call x1, Pallas kernels, shards(): pl.pallas_call(exchange_kernel, in_specs=[pl.BlockSpec(memory_space=pltpu...  86.4 us
    pallas_call x1, Pallas kernels, shards(): pl.pallas_call(local_kernel, grid=(blocks,), in_specs=[pl.BlockSpec(memor...  7.1 us
    unnamed x9, local copies, waits for them, and re-layouts  6.59 us

profile of v1, /device:TPU:1, one launch (start us, length us, event | category | flops | bytes accessed | tf_op | source)
XLA Modules:
  0.0 102.8 jit_solution(15273366731662539473)
XLA Ops:
  0.0 1.2 %slice.3 = s32[1]{0:T(128)} slice(s32[512]{0:T(512)} %param.12), slice={[0:1]} | slice | bytes 8 | tf_op jit(solution)/shard_map/slice | solution.py:382
  1.8 0.8 pad_add_fusion
  2.6 0.1 compare_convert_fusion.keep
  2.7 0.0 copy-start
  2.7 1.6 %copy-done = bf16[1024,1024]{1,0:T(8,128)(2,1)S(1)} copy-done((bf16[1024,1024]{1,0:T(8,128)(2,1)S(1)}, bf16[1024,1024]{1,0:T(8,128)(2,1)}, u32[]{:S(2)}) %copy-start) | copy-done | bytes 2097176
  4.3 0.0 copy-start.1
  4.3 1.2 %copy-done.1 = bf16[1024,512]{1,0:T(8,128)(2,1)S(1)} copy-done((bf16[1024,512]{1,0:T(8,128)(2,1)S(1)}, bf16[1024,512]{1,0:T(8,128)(2,1)}, u32[]{:S(2)}) %copy-start.1) | copy-done | bytes 1048600
  5.5 0.0 copy-start.2
  5.5 1.2 %copy-done.2 = bf16[1024,512]{1,0:T(8,128)(2,1)S(1)} copy-done((bf16[1024,512]{1,0:T(8,128)(2,1)S(1)}, bf16[1024,512]{1,0:T(8,128)(2,1)}, u32[]{:S(2)}) %copy-start.2) | copy-done | bytes 1048600
  6.7 0.0 copy-start.3
  6.7 1.2 %copy-done.3 = bf16[1024,512]{1,0:T(8,128)(2,1)S(1)} copy-done((bf16[1024,512]{1,0:T(8,128)(2,1)S(1)}, bf16[1024,512]{1,0:T(8,128)(2,1)}, u32[]{:S(2)}) %copy-start.3) | copy-done | bytes 1048600
  8.0 7.1 %shard_map.73 = (bf16[1024,1024]{1,0:T(8,128)(2,1)S(1)}, bf16[1024,512]{1,0:T(8,128)(2,1)S(1)}, bf16[256,512]{1,0:T(8,128)(2,1)S(1)}, f32[1,512]{1,0:T(1,128)S(1)}) custom-call(f32[8]{0:T(128)S(1)} %compare_convert_fusion.keep, bf16[1024,512]{1,0:T(8,128)(2,1)S(1)} %copy-done.1, bf16[1024,512]{1,0:T(8,128)(2,1)S(1)} %copy-done.2, ...), custom_call_target="tpu_custom_call" | custom-call | tf_op jit(solution)/shard_map/pallas_call | solution.py:391
  15.1 86.4 %shard_map.74 = bf16[1024,1024]{1,0:T(8,128)(2,1)S(1)} custom-call(bf16[256,512]{1,0:T(8,128)(2,1)S(1)} %get-tuple-element.9.state, f32[1,512]{1,0:T(1,128)S(1)} %get-tuple-element.10.decay, bf16[1024,1024]{1,0:T(8,128)(2,1)S(1)} %get-tuple-element.11.mixed_h, bf16[1024,512]{1,0:T(8,128)(2,1)S(1)} %get-tuple-element.12.reach_h, bf16[1024,1024]{1,0:T(8,128)(2,1)} %gate_h.1, ...), custom_call_target="tpu_custom_call" | custom-call | tf_op jit(solution)/shard_map/pallas_call | solution.py:419
  101.5 1.3 %copy.9 = bf16[1024,1024]{1,0:T(8,128)(2,1)} copy(bf16[1024,1024]{1,0:T(8,128)(2,1)S(1)} %shard_map.74) | data formatting | bytes 4194304
Async XLA Ops:
  2.7 1.6 %copy-start = (bf16[1024,1024]{1,0:T(8,128)(2,1)S(1)}, bf16[1024,1024]{1,0:T(8,128)(2,1)}, u32[]{:S(2)}) copy-start(bf16[1024,1024]{1,0:T(8,128)(2,1)} %v.1) | copy-start | bytes 6291460
  4.3 1.2 %copy-start.1 = (bf16[1024,512]{1,0:T(8,128)(2,1)S(1)}, bf16[1024,512]{1,0:T(8,128)(2,1)}, u32[]{:S(2)}) copy-start(bf16[1024,512]{1,0:T(8,128)(2,1)} %q.1) | copy-start | bytes 3145732
  5.5 1.2 %copy-start.2 = (bf16[1024,512]{1,0:T(8,128)(2,1)S(1)}, bf16[1024,512]{1,0:T(8,128)(2,1)}, u32[]{:S(2)}) copy-start(bf16[1024,512]{1,0:T(8,128)(2,1)} %k.1) | copy-start | bytes 3145732
  6.7 1.2 %copy-start.3 = (bf16[1024,512]{1,0:T(8,128)(2,1)S(1)}, bf16[1024,512]{1,0:T(8,128)(2,1)}, u32[]{:S(2)}) copy-start(bf16[1024,512]{1,0:T(8,128)(2,1)} %g.1) | copy-start | bytes 3145732

commit v2 on v1

--- a/solution.py
+++ b/solution.py
@@ -14,6 +14,7 @@
 
 NX = 4
 NZ = 8
+PIECE = 64
 REACH = 4
 
 
@@ -21,51 +22,9 @@
     return lax.dot_general(a, b, (dims, ((), ())), preferred_element_type=F32)
 
 
-def local_kernel(keep, q, k, v, g, mixed, reach_q, state_out, decay_out, state, weight):
-    b = pl.program_id(0)
-    heads = q.shape[1] // DK
-
-    @pl.when(b == 0)
-    def _():
-        state[...] = jnp.zeros_like(state)
-        weight[...] = jnp.ones_like(weight)
-
-    keep_b = keep[b]
-    rows = lax.broadcasted_iota(jnp.int32, (CH, CH), 0)
-    cols = lax.broadcasted_iota(jnp.int32, (CH, CH), 1)
-    causal = cols <= rows
-    cum = dot(causal.astype(F32).astype(BF16), g[...], ((1,), (0,)))
-    last = cum[CH - 1 : CH, :]
-    qf = q[...].astype(F32)
-    kf = k[...].astype(F32)
-    dq = qf * jnp.exp(cum) * DK ** (-0.5)
-    dk = (kf * jnp.exp(-cum)).astype(BF16)
-    kept = (kf * jnp.exp(last - cum)).astype(BF16)
-    decay = jnp.exp(last)
-    w = weight[...] * keep_b
-    reach_q[...] = (dq * w).astype(BF16)
-    weight[...] = w * decay
-    dq = dq.astype(BF16)
-    for h in range(heads):
-        kc = slice(h * DK, (h + 1) * DK)
-        vc = slice(h * DV, (h + 1) * DV)
-        scores = dot(dq[:, kc], dk[:, kc], ((1,), (1,)))
-        probs = jnp.where(causal, scores, 0.0).astype(BF16)
-        start = state[:, kc] * keep_b
-        out = dot(probs, v[:, vc], ((1,), (0,)))
-        out += dot(dq[:, kc], start.astype(BF16), ((1,), (1,)))
-        mixed[:, vc] = out.astype(BF16)
-        local = dot(v[:, vc], kept[:, kc], ((0,), (0,)))
-        state[:, kc] = start * decay[:, kc] + local
-
-    @pl.when(b == pl.num_programs(0) - 1)
-    def _():
-        state_out[...] = state[...].astype(BF16)
-        decay_out[...] = weight[...]
-
-
-def exchange_kernel(
-    state, decay, mixed_h, reach_h, gate_h, proj_h, out_h,
+def layer_kernel(
+    seg, g_h, k_h, v_h, q_h, gate_h, proj_h, out_h,
+    g, k, v, q, cum, state_f, state, starts, weights, decay,
     mixed, reach, gate, wo, wp, hid, hid_peer, send, recv, res, own,
     p1, a1, xs, acc, t_out, a_out, t_in, a_in, plane, p3, e_in,
     s_p1, r_p1, s_a1, r_a1, s_p2, r_p2, s_a2, r_a2, s_p3, r_p3,
@@ -85,7 +44,9 @@
     xl = (x + NX - 1) % NX
     xo = (x + 2) % NX
     tokens = hid.shape[0]
-    chunks = tokens // CH
+    blocks = tokens // CH
+    chunks = tokens // PIECE
+    heads = reach.shape[1] // DK
     width = wo.shape[2]
     depth = wo.shape[1]
     slab = depth // (2 * NX)
@@ -106,11 +67,13 @@
     mine_cols = pl.ds(pl.multiple_of(y * width, width), width)
     over_cols = pl.ds(pl.multiple_of(over * width, width), width)
     loads = [
-        pltpu.make_async_copy(mixed_h, mixed, s_load.at[0]),
-        pltpu.make_async_copy(reach_h, reach, s_load.at[1]),
-        pltpu.make_async_copy(gate_h, gate, s_load.at[2]),
-        pltpu.make_async_copy(proj_h.at[:, over_cols], wo.at[1], s_load.at[3]),
-        pltpu.make_async_copy(proj_h.at[:, mine_cols], wo.at[0], s_load.at[4]),
+        pltpu.make_async_copy(src, dst, s_load.at[i])
+        for i, (src, dst) in enumerate(
+            (
+                (g_h, g), (k_h, k), (v_h, v), (q_h, q), (gate_h, gate),
+                (proj_h.at[:, over_cols], wo.at[1]), (proj_h.at[:, mine_cols], wo.at[0]),
+            )
+        )
     ]
     for load in loads:
         load.start()
@@ -137,16 +100,6 @@
     ahead = jnp.minimum(NZ - 1 - z, REACH)
     behind = jnp.minimum(z, REACH)
     pl.semaphore_wait(barrier, 2 * NX + 1 + ahead + behind)
-
-    def rows_of(i):
-        return pl.ds(pl.multiple_of(i * part, part), part)
-
-    for step in range(1, 2 * NX):
-        i = (me + step) % (2 * NX)
-        rdma(decay, a1.at[me], s_a1.at[i], r_a1.at[me], base + i, y).start()
-        rdma(state.at[rows_of(i), :], p1.at[me], s_p1.at[i], r_p1.at[me], base + i, y).start()
-    p1[me] = state[rows_of(me), :]
-    a1[me] = decay[...]
 
     def slab_of(xx, cc):
         return pl.ds(pl.multiple_of((xx * 2 + cc) * slab, slab), slab)
@@ -211,6 +164,80 @@
 
     w1(1).start()
     w1(0).start()
+
+    block_rows = lax.broadcasted_iota(jnp.int32, (CH, CH), 0)
+    block_cols = lax.broadcasted_iota(jnp.int32, (CH, CH), 1)
+    causal = block_cols <= block_rows
+    ones = causal.astype(F32).astype(BF16)
+    state_f[...] = jnp.zeros_like(state_f)
+    decay[...] = jnp.ones_like(decay)
+
+    def rows_at(c, size):
+        return pl.ds(pl.multiple_of(c * size, size), size)
+
+    def head_keys(h):
+        return slice(h * DK, (h + 1) * DK)
+
+    def head_vals(h):
+        return slice(h * DV, (h + 1) * DV)
+
+    for load in loads[:3]:
+        load.wait()
+
+    def state_step(b, carry):
+        rows = rows_at(b, CH)
+        at = ctx * blocks + b
+        same = jnp.logical_and(seg[at] == seg[jnp.maximum(at - 1, 0)], at > 0)
+        keep = jnp.where(same, 1.0, 0.0)
+        sums = dot(ones, g[rows, :], ((1,), (0,)))
+        cum[rows, :] = sums
+        last = sums[CH - 1 : CH, :]
+        kept = (k[rows, :].astype(F32) * jnp.exp(last - sums)).astype(BF16)
+        fall = jnp.exp(last)
+        weight = decay[...] * keep
+        weights[b] = weight
+        decay[...] = weight * fall
+        for h in range(heads):
+            kc = head_keys(h)
+            start = state_f[:, kc] * keep
+            starts[b, :, kc] = start.astype(BF16)
+            state_f[:, kc] = start * fall[:, kc] + dot(v[rows, head_vals(h)], kept[:, kc], ((0,), (0,)))
+        return carry
+
+    lax.fori_loop(0, blocks, state_step, 0)
+    state[...] = state_f[...].astype(BF16)
+
+    def rows_of(i):
+        return pl.ds(pl.multiple_of(i * part, part), part)
+
+    for step in range(1, 2 * NX):
+        i = (me + step) % (2 * NX)
+        rdma(decay, a1.at[me], s_a1.at[i], r_a1.at[me], base + i, y).start()
+        rdma(state.at[rows_of(i), :], p1.at[me], s_p1.at[i], r_p1.at[me], base + i, y).start()
+    p1[me] = state[rows_of(me), :]
+    a1[me] = decay[...]
+
+
+    def block_step(b, carry):
+        rows = rows_at(b, CH)
+        sums = cum[rows, :]
+        dq = q[rows, :].astype(F32) * jnp.exp(sums) * DK ** (-0.5)
+        dk = (k[rows, :].astype(F32) * jnp.exp(-sums)).astype(BF16)
+        reach[rows, :] = (dq * weights[b]).astype(BF16)
+        dq = dq.astype(BF16)
+        for h in range(heads):
+            kc = head_keys(h)
+            vc = head_vals(h)
+            scores = dot(dq[:, kc], dk[:, kc], ((1,), (1,)))
+            probs = jnp.where(causal, scores, 0.0).astype(BF16)
+            out = dot(probs, v[rows, vc], ((1,), (0,)))
+            out += dot(dq[:, kc], starts[b, :, kc], ((1,), (1,)))
+            mixed[rows, vc] = out.astype(BF16)
+        return carry
+
+    loads[3].wait()
+    lax.fori_loop(0, blocks // 2, block_step, 0)
+
 
     for step in range(1, 2 * NX):
         i = (me + step) % (2 * NX)
@@ -236,6 +263,7 @@
             rdma(t_out, t_in.at[far - 1], s_p2.at[far - 1], r_p2.at[far - 1], to, y).start()
 
     stage_a(1)
+    lax.fori_loop(blocks // 2, blocks, block_step, 0)
 
     plane[...] = jnp.zeros_like(plane)
     for far in range(REACH, 0, -1):
@@ -253,24 +281,18 @@
         rdma(p3.at[i], e_in.at[rows_of(me), :], s_p3.at[i], r_p3.at[me], base + i, y).start()
     e_in[rows_of(me), :] = p3[me]
 
-    for load in loads[:3]:
-        load.wait()
+    loads[4].wait()
     stage_b(1)
 
     for step in range(1, 2 * NX):
         i = (me + step) % (2 * NX)
         arrived(e_in.at[rows_of(i), :], s_p3.at[i], r_p3.at[i])
 
-    heads = reach.shape[1] // DK
-
-    def chunk_rows(c):
-        return pl.ds(pl.multiple_of(c * CH, CH), CH)
-
     def hidden_step(c, carry):
-        rows = chunk_rows(c)
+        rows = rows_at(c, PIECE)
         for h in range(heads):
-            kc = slice(h * DK, (h + 1) * DK)
-            vc = slice(h * DV, (h + 1) * DV)
+            kc = head_keys(h)
+            vc = head_vals(h)
             full = mixed[rows, vc].astype(F32)
             full += dot(reach[rows, kc], e_in[:, kc], ((1,), (1,)))
             mean = jnp.mean(full * full, axis=-1, keepdims=True)
@@ -284,7 +306,7 @@
 
     stage_c(1)
     stage_a(0)
-    for load in loads[3:]:
+    for load in loads[5:]:
         load.wait()
     stage_d(1)
 
@@ -300,7 +322,7 @@
     def main_step(c, carry):
         @pl.when(c < chunks)
         def _():
-            rows = chunk_rows(c)
+            rows = rows_at(c, PIECE)
             arrived(hid_peer.at[rows, :], s_hid.at[c], r_hid.at[c])
 
             def column(n, carry):
@@ -326,7 +348,7 @@
         @pl.when(c >= lag)
         def _():
             d = c - lag
-            rows = chunk_rows(d)
+            rows = rows_at(d, PIECE)
 
             def column(n, carry):
                 total, cols = product(rows, 0, n)
@@ -358,7 +380,7 @@
     weights_left(0)
 
     def finish(c, carry):
-        rows = chunk_rows(c)
+        rows = rows_at(c, PIECE)
         left(hid.at[rows, :], s_hid.at[c], r_hid.at[c])
         left(send.at[rows, :], s_rs.at[c], r_rs.at[c])
         pltpu.make_async_copy(res.at[rows, :], out_h.at[rows, :], s_out.at[c]).wait()
@@ -371,57 +393,31 @@
     tokens = queries.shape[0]
     keys_wide = queries.shape[1]
     vals_wide = values.shape[1]
-    blocks = tokens // CH
     depth, full = final_projector.shape
     width = full // 4
     slots = 2 * NX
     part = DV // slots
-    chunks = tokens // CH
-
-    first_block = lax.axis_index("ctx") * blocks
-    padded = jnp.concatenate([segment_ids[:1] - 1, segment_ids])
-    current = lax.dynamic_slice_in_dim(padded, first_block + 1, blocks)
-    before = lax.dynamic_slice_in_dim(padded, first_block, blocks)
-    keep = (current == before).astype(F32)
-
-    def by_block(wide):
-        return pl.BlockSpec((CH, wide), lambda b: (b, 0))
-
-    whole = lambda b: (0, 0)
-    mixed, reach, state, decay = pl.pallas_call(
-        local_kernel,
-        grid=(blocks,),
-        in_specs=[
-            pl.BlockSpec(memory_space=pltpu.SMEM),
-            by_block(keys_wide),
-            by_block(keys_wide),
-            by_block(vals_wide),
-            by_block(keys_wide),
-        ],
-        out_specs=[
-            by_block(vals_wide),
-            by_block(keys_wide),
-            pl.BlockSpec((DV, keys_wide), whole),
-            pl.BlockSpec((1, keys_wide), whole),
-        ],
-        out_shape=[
-            jax.ShapeDtypeStruct((tokens, vals_wide), BF16),
-            jax.ShapeDtypeStruct((tokens, keys_wide), BF16),
-            jax.ShapeDtypeStruct((DV, keys_wide), BF16),
-            jax.ShapeDtypeStruct((1, keys_wide), F32),
-        ],
-        scratch_shapes=[pltpu.VMEM((DV, keys_wide), F32), pltpu.VMEM((1, keys_wide), F32)],
-        compiler_params=pltpu.CompilerParams(vmem_limit_bytes=32 * 2**20),
-    )(keep, queries, keys, values, log_gate)
+    blocks = tokens // CH
+    chunks = tokens // PIECE
 
     vm = pltpu.VMEM
     dma = pltpu.SemaphoreType.DMA
     return pl.pallas_call(
-        exchange_kernel,
-        in_specs=[pl.BlockSpec(memory_space=pltpu.VMEM)] * 2 + [pl.BlockSpec(memory_space=pl.ANY)] * 4,
+        layer_kernel,
+        in_specs=[pl.BlockSpec(memory_space=pltpu.SMEM)] + [pl.BlockSpec(memory_space=pl.ANY)] * 6,
         out_specs=pl.BlockSpec(memory_space=pl.ANY),
         out_shape=jax.ShapeDtypeStruct((tokens, width), BF16),
         scratch_shapes=[
+            vm((tokens, keys_wide), BF16),
+            vm((tokens, keys_wide), BF16),
+            vm((tokens, vals_wide), BF16),
+            vm((tokens, keys_wide), BF16),
+            vm((tokens, keys_wide), F32),
+            vm((DV, keys_wide), F32),
+            vm((DV, keys_wide), BF16),
+            vm((blocks, DV, keys_wide), BF16),
+            vm((blocks, 1, keys_wide), F32),
+            vm((1, keys_wide), F32),
             vm((tokens, vals_wide), BF16),
             vm((tokens, keys_wide), BF16),
             vm((tokens, vals_wide), BF16),
@@ -432,7 +428,7 @@
             vm((tokens, width), BF16),
             vm((tokens, width), BF16),
             vm((tokens, width), BF16),
-            vm((CH, width), F32),
+            vm((PIECE, width), F32),
             vm((slots, part, keys_wide), BF16),
             vm((slots, 1, keys_wide), F32),
             vm((slots, part, keys_wide), F32),
@@ -455,13 +451,13 @@
             dma((2, 5)), dma((2, 5)),
             dma((chunks,)), dma((chunks,)),
             dma((chunks,)), dma((chunks,)),
-            dma((5,)),
+            dma((7,)),
             dma((chunks,)),
         ],
         compiler_params=pltpu.CompilerParams(
-            collective_id=0, has_side_effects=True, vmem_limit_bytes=48 * 2**20
+            collective_id=0, has_side_effects=True, vmem_limit_bytes=56 * 2**20
         ),
-    )(state, decay, mixed, reach, out_gate, final_projector)
+    )(segment_ids, log_gate, keys, values, queries, out_gate, final_projector)
 
 
 def solution(mesh):

time: 103 us -> 96.7 us (0.939)
  local copies, waits for them, and re-layouts: 7.78 us -> 3.08 us
    unnamed x9 -> x1, local copies, waits for them, and re-layouts: 6.59 us -> 3.08 us
    slice x1 -> x0, local copies, waits for them, and re-layouts: 1.19 us -> none  [shards(): padded = jnp.concatenate([segment_ids[:1] - 1, segment_ids])]
    pallas_call x2 -> x1, Pallas kernels: 93.5 us -> 93.5 us  [shards(): pl.pallas_call(layer_kernel, in_specs=[pl.BlockSpec(memory_space=pltpu.SM...]
where the time goes in v2:
time: 96.7 us; the launch traced here: 96.6 us
  Pallas kernels  93.5 us (97%)
  local copies, waits for them, and re-layouts  3.08 us (3%)
    pallas_call x1, Pallas kernels, shards(): pl.pallas_call(layer_kernel, in_specs=[pl.BlockSpec(memory_space=pltpu.SM...  93.5 us
    unnamed x1, local copies, waits for them, and re-layouts  3.08 us

profile of v2, /device:TPU:1, one launch (start us, length us, event | category | flops | bytes accessed | tf_op | source)
XLA Modules:
  0.0 96.6 jit_solution(16369221285463178208)
XLA Ops:
  0.0 93.5 %shard_map.73 = bf16[1024,1024]{1,0:T(8,128)(2,1)} custom-call(s32[512]{0:T(512)} %seg.1, bf16[1024,512]{1,0:T(8,128)(2,1)} %g_h.1, bf16[1024,512]{1,0:T(8,128)(2,1)} %k_h.1, bf16[1024,1024]{1,0:T(8,128)(2,1)} %v_h.1, bf16[1024,512]{1,0:T(8,128)(2,1)} %q_h.1, bf16[1024,1024]{1,0:T(8,128)(2,1)} %gate_h.1, bf16[1024,4096]{1,0:T(8,128)(2,1)} %proj_h.1), custom_call_target="tpu_custom_call" | custom-call | tf_op jit(solution)/shard_map/pallas_call | solution.py:405
  93.5 3.1 %copy.9 = bf16[1024,1024]{1,0:T(8,128)(2,1)} copy(bf16[1024,1024]{1,0:T(8,128)(2,1)} %shard_map.73) | data formatting | bytes 4194304

commit v3 on v2

--- a/solution.py
+++ b/solution.py
@@ -25,7 +25,7 @@
 def layer_kernel(
     seg, g_h, k_h, v_h, q_h, gate_h, proj_h, out_h,
     g, k, v, q, cum, state_f, state, starts, weights, decay,
-    mixed, reach, gate, wo, wp, hid, hid_peer, send, recv, res, own,
+    mixed, reach, gate, wo, wp, hid, hid_peer, send, recv, res, own, ahead_of,
     p1, a1, xs, acc, t_out, a_out, t_in, a_in, plane, p3, e_in,
     s_p1, r_p1, s_a1, r_a1, s_p2, r_p2, s_a2, r_a2, s_p3, r_p3,
     s_w1, r_w1, s_wx, r_wx, s_wf, r_wf, s_ws, r_ws,
@@ -50,7 +50,7 @@
     width = wo.shape[2]
     depth = wo.shape[1]
     slab = depth // (2 * NX)
-    part = p1.shape[1]
+    part = p1.shape[2]
 
     def rdma(src, dst, ssem, rsem, c, h):
         return pltpu.make_async_remote_copy(
@@ -171,6 +171,9 @@
     ones = causal.astype(F32).astype(BF16)
     state_f[...] = jnp.zeros_like(state_f)
     decay[...] = jnp.ones_like(decay)
+    wide = p1.shape[3]
+    halves = p1.shape[0]
+    group = heads // halves
 
     def rows_at(c, size):
         return pl.ds(pl.multiple_of(c * size, size), size)
@@ -184,39 +187,46 @@
     for load in loads[:3]:
         load.wait()
 
-    def state_step(b, carry):
+    def state_step(f, b):
+        lanes = slice(f * wide, (f + 1) * wide)
         rows = rows_at(b, CH)
         at = ctx * blocks + b
         same = jnp.logical_and(seg[at] == seg[jnp.maximum(at - 1, 0)], at > 0)
         keep = jnp.where(same, 1.0, 0.0)
-        sums = dot(ones, g[rows, :], ((1,), (0,)))
-        cum[rows, :] = sums
+        sums = dot(ones, g[rows, lanes], ((1,), (0,)))
+        cum[rows, lanes] = sums
         last = sums[CH - 1 : CH, :]
-        kept = (k[rows, :].astype(F32) * jnp.exp(last - sums)).astype(BF16)
+        kept = (k[rows, lanes].astype(F32) * jnp.exp(last - sums)).astype(BF16)
         fall = jnp.exp(last)
-        weight = decay[...] * keep
-        weights[b] = weight
-        decay[...] = weight * fall
-        for h in range(heads):
-            kc = head_keys(h)
-            start = state_f[:, kc] * keep
-            starts[b, :, kc] = start.astype(BF16)
-            state_f[:, kc] = start * fall[:, kc] + dot(v[rows, head_vals(h)], kept[:, kc], ((0,), (0,)))
-        return carry
-
-    lax.fori_loop(0, blocks, state_step, 0)
-    state[...] = state_f[...].astype(BF16)
+        weight = decay[f] * keep
+        weights[b, :, lanes] = weight
+        decay[f] = weight * fall
+        for i in range(group):
+            kc = head_keys(i)
+            start = state_f[f, :, kc] * keep
+            starts[b, :, head_keys(f * group + i)] = start.astype(BF16)
+            added = dot(v[rows, head_vals(f * group + i)], kept[:, kc], ((0,), (0,)))
+            state_f[f, :, kc] = start * fall[:, kc] + added
 
     def rows_of(i):
         return pl.ds(pl.multiple_of(i * part, part), part)
 
-    for step in range(1, 2 * NX):
-        i = (me + step) % (2 * NX)
-        rdma(decay, a1.at[me], s_a1.at[i], r_a1.at[me], base + i, y).start()
-        rdma(state.at[rows_of(i), :], p1.at[me], s_p1.at[i], r_p1.at[me], base + i, y).start()
-    p1[me] = state[rows_of(me), :]
-    a1[me] = decay[...]
-
+    for f in range(halves):
+
+        def step_of(b, carry):
+            state_step(f, b)
+            return carry
+
+        lax.fori_loop(0, blocks, step_of, 0)
+        state[f] = state_f[f].astype(BF16)
+        for step in range(1, 2 * NX):
+            i = (me + step) % (2 * NX)
+            rdma(decay.at[f], a1.at[f, me], s_a1.at[f, i], r_a1.at[f, me], base + i, y).start()
+            rdma(
+                state.at[f, rows_of(i), :], p1.at[f, me], s_p1.at[f, i], r_p1.at[f, me], base + i, y
+            ).start()
+        p1[f, me] = state[f, rows_of(me), :]
+        a1[f, me] = decay[f]
 
     def block_step(b, carry):
         rows = rows_at(b, CH)
@@ -239,54 +249,59 @@
     lax.fori_loop(0, blocks // 2, block_step, 0)
 
 
-    for step in range(1, 2 * NX):
-        i = (me + step) % (2 * NX)
-        arrived(a1.at[i], s_a1.at[i], r_a1.at[i])
-        arrived(p1.at[i], s_p1.at[i], r_p1.at[i])
-
-    run = jnp.zeros((part, p1.shape[2]), F32)
-    scale = jnp.ones((1, p1.shape[2]), F32)
-    for i in range(2 * NX):
-        xs[i] = run
-        acc[i] = scale
-        run = run * a1[i] + p1[i].astype(F32)
-        scale = scale * a1[i]
-    t_out[...] = run.astype(BF16)
-    a_out[...] = scale
-
-    for far in range(1, REACH + 1):
-
-        @pl.when(z + far < NZ)
-        def _():
-            to = ctx + far * 2 * NX
-            rdma(a_out, a_in.at[far - 1], s_a2.at[far - 1], r_a2.at[far - 1], to, y).start()
-            rdma(t_out, t_in.at[far - 1], s_p2.at[far - 1], r_p2.at[far - 1], to, y).start()
+    for f in range(halves):
+        for step in range(1, 2 * NX):
+            i = (me + step) % (2 * NX)
+            arrived(a1.at[f, i], s_a1.at[f, i], r_a1.at[f, i])
+            arrived(p1.at[f, i], s_p1.at[f, i], r_p1.at[f, i])
+        run = jnp.zeros((part, wide), F32)
+        scale = jnp.ones((1, wide), F32)
+        for i in range(2 * NX):
+            xs[f, i] = run
+            acc[f, i] = scale
+            run = run * a1[f, i] + p1[f, i].astype(F32)
+            scale = scale * a1[f, i]
+        t_out[f] = run.astype(BF16)
+        a_out[f] = scale
+        for far in range(1, REACH + 1):
+
+            @pl.when(z + far < NZ)
+            def _():
+                to = ctx + far * 2 * NX
+                n = far - 1
+                rdma(a_out.at[f], a_in.at[f, n], s_a2.at[f, n], r_a2.at[f, n], to, y).start()
+                rdma(t_out.at[f], t_in.at[f, n], s_p2.at[f, n], r_p2.at[f, n], to, y).start()
 
     stage_a(1)
     lax.fori_loop(blocks // 2, blocks, block_step, 0)
 
-    plane[...] = jnp.zeros_like(plane)
-    for far in range(REACH, 0, -1):
-
-        @pl.when(z - far >= 0)
-        def _():
-            arrived(a_in.at[far - 1], s_a2.at[far - 1], r_a2.at[far - 1])
-            arrived(t_in.at[far - 1], s_p2.at[far - 1], r_p2.at[far - 1])
-            plane[...] = plane[...] * a_in[far - 1] + t_in[far - 1].astype(F32)
-
-    for i in range(2 * NX):
-        p3[i] = (xs[i] + acc[i] * plane[...]).astype(BF16)
-    for step in range(1, 2 * NX):
-        i = (me + step) % (2 * NX)
-        rdma(p3.at[i], e_in.at[rows_of(me), :], s_p3.at[i], r_p3.at[me], base + i, y).start()
-    e_in[rows_of(me), :] = p3[me]
+    for f in range(halves):
+        plane[...] = jnp.zeros_like(plane)
+        for far in range(REACH, 0, -1):
+
+            @pl.when(z - far >= 0)
+            def _():
+                n = far - 1
+                arrived(a_in.at[f, n], s_a2.at[f, n], r_a2.at[f, n])
+                arrived(t_in.at[f, n], s_p2.at[f, n], r_p2.at[f, n])
+                plane[...] = plane[...] * a_in[f, n] + t_in[f, n].astype(F32)
+
+        for i in range(2 * NX):
+            p3[f, i] = (xs[f, i] + acc[f, i] * plane[...]).astype(BF16)
+        for step in range(1, 2 * NX):
+            i = (me + step) % (2 * NX)
+            rdma(
+                p3.at[f, i], e_in.at[f, rows_of(me), :], s_p3.at[f, i], r_p3.at[f, me], base + i, y
+            ).start()
+        e_in[f, rows_of(me), :] = p3[f, me]
 
     loads[4].wait()
     stage_b(1)
 
-    for step in range(1, 2 * NX):
-        i = (me + step) % (2 * NX)
-        arrived(e_in.at[rows_of(i), :], s_p3.at[i], r_p3.at[i])
+    for f in range(halves):
+        for step in range(1, 2 * NX):
+            i = (me + step) % (2 * NX)
+            arrived(e_in.at[f, rows_of(i), :], s_p3.at[f, i], r_p3.at[f, i])
 
     def hidden_step(c, carry):
         rows = rows_at(c, PIECE)
@@ -294,7 +309,7 @@
             kc = head_keys(h)
             vc = head_vals(h)
             full = mixed[rows, vc].astype(F32)
-            full += dot(reach[rows, kc], e_in[:, kc], ((1,), (1,)))
+            full += dot(reach[rows, kc], e_in[h // group, :, head_keys(h % group)], ((1,), (1,)))
             mean = jnp.mean(full * full, axis=-1, keepdims=True)
             val = gate[rows, vc].astype(F32)
             silu = val / (1.0 + jnp.exp(-val))
@@ -312,32 +327,38 @@
 
     tile = 512
 
-    def product(rows, j, n):
-        cols = pl.ds(pl.multiple_of(n * tile, tile), tile)
-        total = dot(hid[rows, :], wo[j, :, cols], ((1,), (0,)))
-        return total + dot(hid_peer[rows, :], wp[j, :, cols], ((1,), (0,))), cols
-
-    lag = 2
+    def columns(do):
+        def column(n, carry):
+            do(pl.ds(pl.multiple_of(n * tile, tile), tile))
+            return carry
+
+        lax.fori_loop(0, width // tile, column, 0)
+
+    lag = 8
+    pieces = CH // PIECE
 
     def main_step(c, carry):
         @pl.when(c < chunks)
         def _():
             rows = rows_at(c, PIECE)
+
+            def own_part(cols):
+                ahead_of[:, cols] = dot(hid[rows, :], wo[1, :, cols], ((1,), (0,)))
+
+            def pair_part(cols):
+                total = ahead_of[:, cols] + dot(hid_peer[rows, :], wp[1, :, cols], ((1,), (0,)))
+                send[rows, cols] = total.astype(BF16)
+
+            columns(own_part)
             arrived(hid_peer.at[rows, :], s_hid.at[c], r_hid.at[c])
-
-            def column(n, carry):
-                total, cols = product(rows, 1, n)
-                send[rows, cols] = total.astype(BF16)
-                return carry
-
-            lax.fori_loop(0, width // tile, column, 0)
+            columns(pair_part)
             rdma(send.at[rows, :], recv.at[rows, :], s_rs.at[c], r_rs.at[c], ctx, over).start()
 
-        @pl.when(c == 0)
+        @pl.when(c == 3)
         def _():
             stage_b(0)
 
-        @pl.when(c == 1)
+        @pl.when(c == 5)
         def _():
             stage_c(0)
 
@@ -348,33 +369,37 @@
         @pl.when(c >= lag)
         def _():
             d = c - lag
-            rows = rows_at(d, PIECE)
-
-            def column(n, carry):
-                total, cols = product(rows, 0, n)
-                own[:, cols] = total
-                return carry
-
-            lax.fori_loop(0, width // tile, column, 0)
-            arrived(recv.at[rows, :], s_rs.at[d], r_rs.at[d])
+            rows = rows_at(d, CH)
+
+            def both_parts(cols):
+                total = dot(hid[rows, :], wo[0, :, cols], ((1,), (0,)))
+                own[:, cols] = total + dot(hid_peer[rows, :], wp[0, :, cols], ((1,), (0,)))
+
+            columns(both_parts)
+            for piece in range(pieces):
+                got = rows_at(d * pieces + piece, PIECE)
+                n = d * pieces + piece
+                arrived(recv.at[got, :], s_rs.at[n], r_rs.at[n])
             res[rows, :] = (own[...] + recv[rows, :].astype(F32)).astype(BF16)
             pltpu.make_async_copy(res.at[rows, :], out_h.at[rows, :], s_out.at[d]).start()
 
         return carry
 
-    lax.fori_loop(0, chunks + lag, main_step, 0)
-
-    for step in range(1, 2 * NX):
-        i = (me + step) % (2 * NX)
-        left(decay, s_a1.at[i], r_a1.at[i])
-        left(p1.at[i], s_p1.at[i], r_p1.at[i])
-        left(p3.at[i], s_p3.at[i], r_p3.at[i])
-    for far in range(1, REACH + 1):
-
-        @pl.when(z + far < NZ)
-        def _():
-            left(a_out, s_a2.at[far - 1], r_a2.at[far - 1])
-            left(t_out, s_p2.at[far - 1], r_p2.at[far - 1])
+    lax.fori_loop(0, lag + blocks, main_step, 0)
+
+    for f in range(halves):
+        for step in range(1, 2 * NX):
+            i = (me + step) % (2 * NX)
+            left(decay.at[f], s_a1.at[f, i], r_a1.at[f, i])
+            left(p1.at[f, i], s_p1.at[f, i], r_p1.at[f, i])
+            left(p3.at[f, i], s_p3.at[f, i], r_p3.at[f, i])
+        for far in range(1, REACH + 1):
+
+            @pl.when(z + far < NZ)
+            def _():
+                n = far - 1
+                left(a_out.at[f], s_a2.at[f, n], r_a2.at[f, n])
+                left(t_out.at[f], s_p2.at[f, n], r_p2.at[f, n])
 
     weights_left(1)
     weights_left(0)
@@ -383,10 +408,12 @@
         rows = rows_at(c, PIECE)
         left(hid.at[rows, :], s_hid.at[c], r_hid.at[c])
         left(send.at[rows, :], s_rs.at[c], r_rs.at[c])
-        pltpu.make_async_copy(res.at[rows, :], out_h.at[rows, :], s_out.at[c]).wait()
         return carry
 
     lax.fori_loop(0, chunks, finish, 0)
+    for d in range(blocks):
+        rows = rows_at(d, CH)
+        pltpu.make_async_copy(res.at[rows, :], out_h.at[rows, :], s_out.at[d]).wait()
 
 
 def shards(queries, keys, values, log_gate, out_gate, segment_ids, final_projector):
@@ -399,6 +426,8 @@
     part = DV // slots
     blocks = tokens // CH
     chunks = tokens // PIECE
+    halves = 2
+    wide = keys_wide // halves
 
     vm = pltpu.VMEM
     dma = pltpu.SemaphoreType.DMA
@@ -413,11 +442,11 @@
             vm((tokens, vals_wide), BF16),
             vm((tokens, keys_wide), BF16),
             vm((tokens, keys_wide), F32),
-            vm((DV, keys_wide), F32),
-            vm((DV, keys_wide), BF16),
+            vm((halves, DV, wide), F32),
+            vm((halves, DV, wide), BF16),
             vm((blocks, DV, keys_wide), BF16),
             vm((blocks, 1, keys_wide), F32),
-            vm((1, keys_wide), F32),
+            vm((halves, 1, wide), F32),
             vm((tokens, vals_wide), BF16),
             vm((tokens, keys_wide), BF16),
             vm((tokens, vals_wide), BF16),
@@ -428,23 +457,24 @@
             vm((tokens, width), BF16),
             vm((tokens, width), BF16),
             vm((tokens, width), BF16),
+            vm((CH, width), F32),
             vm((PIECE, width), F32),
-            vm((slots, part, keys_wide), BF16),
-            vm((slots, 1, keys_wide), F32),
-            vm((slots, part, keys_wide), F32),
-            vm((slots, 1, keys_wide), F32),
-            vm((part, keys_wide), BF16),
-            vm((1, keys_wide), F32),
-            vm((REACH, part, keys_wide), BF16),
-            vm((REACH, 1, keys_wide), F32),
-            vm((part, keys_wide), F32),
-            vm((slots, part, keys_wide), BF16),
-            vm((DV, keys_wide), BF16),
-            dma((slots,)), dma((slots,)),
-            dma((slots,)), dma((slots,)),
-            dma((REACH,)), dma((REACH,)),
-            dma((REACH,)), dma((REACH,)),
-            dma((slots,)), dma((slots,)),
+            vm((halves, slots, part, wide), BF16),
+            vm((halves, slots, 1, wide), F32),
+            vm((halves, slots, part, wide), F32),
+            vm((halves, slots, 1, wide), F32),
+            vm((halves, part, wide), BF16),
+            vm((halves, 1, wide), F32),
+            vm((halves, REACH, part, wide), BF16),
+            vm((halves, REACH, 1, wide), F32),
+            vm((part, wide), F32),
+            vm((halves, slots, part, wide), BF16),
+            vm((halves, DV, wide), BF16),
+            dma((halves, slots)), dma((halves, slots)),
+            dma((halves, slots)), dma((halves, slots)),
+            dma((halves, REACH)), dma((halves, REACH)),
+            dma((halves, REACH)), dma((halves, REACH)),
+            dma((halves, slots)), dma((halves, slots)),
             dma((2,)), dma((2,)),
             dma((2, 2)), dma((2, 2)),
             dma((2, 2)), dma((2, 2)),
@@ -452,7 +482,7 @@
             dma((chunks,)), dma((chunks,)),
             dma((chunks,)), dma((chunks,)),
             dma((7,)),
-            dma((chunks,)),
+            dma((blocks,)),
         ],
         compiler_params=pltpu.CompilerParams(
             collective_id=0, has_side_effects=True, vmem_limit_bytes=56 * 2**20

time: 96.7 us -> 92.9 us (0.961)
  Pallas kernels: 93.5 us -> 89.7 us
    pallas_call x1, Pallas kernels: 93.5 us -> 89.7 us  [shards(): pl.pallas_call(layer_kernel, in_specs=[pl.BlockSpec(memory_space=pltpu.SM...]
where the time goes in v3:
time: 92.9 us; the launch traced here: 92.8 us
  Pallas kernels  89.7 us (97%)
  local copies, waits for them, and re-layouts  3.08 us (3%)
    pallas_call x1, Pallas kernels, shards(): pl.pallas_call(layer_kernel, in_specs=[pl.BlockSpec(memory_space=pltpu.SM...  89.7 us
    unnamed x1, local copies, waits for them, and re-layouts  3.08 us

profile of v3, /device:TPU:1, one launch (start us, length us, event | category | flops | bytes accessed | tf_op | source)
XLA Modules:
  0.0 92.8 jit_solution(12243827495970717777)
XLA Ops:
  0.0 89.7 %shard_map.73 = bf16[1024,1024]{1,0:T(8,128)(2,1)} custom-call(s32[512]{0:T(512)} %seg.1, bf16[1024,512]{1,0:T(8,128)(2,1)} %g_h.1, bf16[1024,512]{1,0:T(8,128)(2,1)} %k_h.1, bf16[1024,1024]{1,0:T(8,128)(2,1)} %v_h.1, bf16[1024,512]{1,0:T(8,128)(2,1)} %q_h.1, bf16[1024,1024]{1,0:T(8,128)(2,1)} %gate_h.1, bf16[1024,4096]{1,0:T(8,128)(2,1)} %proj_h.1), custom_call_target="tpu_custom_call" | custom-call | tf_op jit(solution)/shard_map/pallas_call | solution.py:434
  89.7 3.1 %copy.9 = bf16[1024,1024]{1,0:T(8,128)(2,1)} copy(bf16[1024,1024]{1,0:T(8,128)(2,1)} %shard_map.73) | data formatting | bytes 4194304

commit v4 on v3

--- a/solution.py
+++ b/solution.py
@@ -15,6 +15,7 @@
 NX = 4
 NZ = 8
 PIECE = 64
+CROSS = 2
 REACH = 4
 
 
@@ -40,6 +41,7 @@
     base = z * (2 * NX)
     pair = y + 1 - 2 * (y % 2)
     over = 3 - y
+    over_pair = over + 1 - 2 * (over % 2)
     xr = (x + 1) % NX
     xl = (x + NX - 1) % NX
     xo = (x + 2) % NX
@@ -66,12 +68,14 @@
 
     mine_cols = pl.ds(pl.multiple_of(y * width, width), width)
     over_cols = pl.ds(pl.multiple_of(over * width, width), width)
+    pair_cols = pl.ds(pl.multiple_of(pair * width, width), width)
     loads = [
         pltpu.make_async_copy(src, dst, s_load.at[i])
         for i, (src, dst) in enumerate(
             (
                 (g_h, g), (k_h, k), (v_h, v), (q_h, q), (gate_h, gate),
                 (proj_h.at[:, over_cols], wo.at[1]), (proj_h.at[:, mine_cols], wo.at[0]),
+                (proj_h.at[:, pair_cols], wo.at[2]),
             )
         )
     ]
@@ -101,69 +105,81 @@
     behind = jnp.minimum(z, REACH)
     pl.semaphore_wait(barrier, 2 * NX + 1 + ahead + behind)
 
-    def slab_of(xx, cc):
-        return pl.ds(pl.multiple_of((xx * 2 + cc) * slab, slab), slab)
-
-    def half_of(xx, cc, half):
-        return pl.ds(pl.multiple_of((xx * 2 + cc) * slab + half * (slab // 2), slab // 2), slab // 2)
-
-    pair_cols = (
-        pl.ds(pl.multiple_of(pair * width, width), width),
-        pl.ds(pl.multiple_of((3 - pair) * width, width), width),
+    units = (
+        (1, 0, slab // 2, pair, 3 - pair),
+        (1, slab // 2, slab // 2, pair, 3 - pair),
+        (0, 0, slab, pair, pair),
+        (3, 0, slab, over, over_pair),
+        (2, 0, slab, over, over),
     )
-    here = slab_of(x, core)
+
+    def unit_rows(u, xx, cc, half=None):
+        _, first, size, _, _ = units[u]
+        if half is not None:
+            size = size // 2
+            first = first + half * size
+        return pl.ds(pl.multiple_of((xx * 2 + cc) * slab + first, size), size)
+
     at_r = base + xr * 2 + core
     at_l = base + xl * 2 + core
     sib = base + x * 2 + 1 - core
 
-    def w1(j):
-        return rdma(proj_h.at[here, pair_cols[j]], wp.at[j, here], s_w1.at[j], r_w1.at[j], ctx, pair)
-
-    def along(j, rows, s, r, item, to):
-        return rdma(wp.at[j, rows], wp.at[j, rows], s.at[j, item], r.at[j, item], to, y)
-
-    def wait_in(j, rows, s, r, item):
-        arrived(wp.at[j, rows], s.at[j, item], r.at[j, item])
-
-    def relays(cc):
+    def w1(u):
+        j, _, _, to, block = units[u]
+        rows = unit_rows(u, x, core)
+        cols = pl.ds(pl.multiple_of(block * width, width), width)
+        return rdma(proj_h.at[rows, cols], wp.at[j, rows], s_w1.at[u], r_w1.at[u], ctx, to)
+
+    def along(u, rows, s, r, item, to):
+        j = units[u][0]
+        return rdma(wp.at[j, rows], wp.at[j, rows], s.at[u, item], r.at[u, item], to, y)
+
+    def wait_in(u, rows, s, r, item):
+        arrived(wp.at[units[u][0], rows], s.at[u, item], r.at[u, item])
+
+    def relays(u, cc):
         return (
-            slab_of(x, cc), slab_of(xl, cc), slab_of(xr, cc), half_of(xo, cc, 0), half_of(xo, cc, 1),
+            unit_rows(u, x, cc), unit_rows(u, xl, cc), unit_rows(u, xr, cc),
+            unit_rows(u, xo, cc, 0), unit_rows(u, xo, cc, 1),
         )
 
-    def stage_a(j):
-        arrived(wp.at[j, here], s_w1.at[j], r_w1.at[j])
-        along(j, here, s_wx, r_wx, 0, at_r).start()
-        along(j, here, s_wx, r_wx, 1, at_l).start()
-        along(j, here, s_ws, r_ws, 0, sib).start()
-
-    def stage_b(j):
-        wait_in(j, slab_of(xl, core), s_wx, r_wx, 0)
-        along(j, half_of(xl, core, 0), s_wf, r_wf, 0, at_r).start()
-        along(j, slab_of(xl, core), s_ws, r_ws, 1, sib).start()
-        wait_in(j, slab_of(xr, core), s_wx, r_wx, 1)
-        along(j, half_of(xr, core, 1), s_wf, r_wf, 1, at_l).start()
-        along(j, slab_of(xr, core), s_ws, r_ws, 2, sib).start()
-
-    def stage_c(j):
-        wait_in(j, half_of(xo, core, 0), s_wf, r_wf, 0)
-        along(j, half_of(xo, core, 0), s_ws, r_ws, 3, sib).start()
-        wait_in(j, half_of(xo, core, 1), s_wf, r_wf, 1)
-        along(j, half_of(xo, core, 1), s_ws, r_ws, 4, sib).start()
-
-    def stage_d(j):
-        for item, rows in enumerate(relays(1 - core)):
-            wait_in(j, rows, s_ws, r_ws, item)
-
-    def weights_left(j):
-        left(wp.at[j, here], s_w1.at[j], r_w1.at[j])
+    def stage_a(u):
+        here = unit_rows(u, x, core)
+        arrived(wp.at[units[u][0], here], s_w1.at[u], r_w1.at[u])
+        along(u, here, s_wx, r_wx, 0, at_r).start()
+        along(u, here, s_wx, r_wx, 1, at_l).start()
+        along(u, here, s_ws, r_ws, 0, sib).start()
+
+    def stage_b(u):
+        wait_in(u, unit_rows(u, xl, core), s_wx, r_wx, 0)
+        along(u, unit_rows(u, xl, core, 0), s_wf, r_wf, 0, at_r).start()
+        along(u, unit_rows(u, xl, core), s_ws, r_ws, 1, sib).start()
+        wait_in(u, unit_rows(u, xr, core), s_wx, r_wx, 1)
+        along(u, unit_rows(u, xr, core, 1), s_wf, r_wf, 1, at_l).start()
+        along(u, unit_rows(u, xr, core), s_ws, r_ws, 2, sib).start()
+
+    def stage_c(u):
+        wait_in(u, unit_rows(u, xo, core, 0), s_wf, r_wf, 0)
+        along(u, unit_rows(u, xo, core, 0), s_ws, r_ws, 3, sib).start()
+        wait_in(u, unit_rows(u, xo, core, 1), s_wf, r_wf, 1)
+        along(u, unit_rows(u, xo, core, 1), s_ws, r_ws, 4, sib).start()
+
+    def stage_d(u):
+        for item, rows in enumerate(relays(u, 1 - core)):
+            wait_in(u, rows, s_ws, r_ws, item)
+
+    def weights_left(u):
+        j = units[u][0]
+        here = unit_rows(u, x, core)
+        left(wp.at[j, here], s_w1.at[u], r_w1.at[u])
         for item in range(2):
-            left(wp.at[j, here], s_wx.at[j, item], r_wx.at[j, item])
-            left(wp.at[j, half_of(x, core, 0)], s_wf.at[j, item], r_wf.at[j, item])
-        for item, rows in enumerate(relays(core)):
-            left(wp.at[j, rows], s_ws.at[j, item], r_ws.at[j, item])
-
-    w1(1).start()
-    w1(0).start()
+            left(wp.at[j, here], s_wx.at[u, item], r_wx.at[u, item])
+            left(wp.at[j, unit_rows(u, x, core, 0)], s_wf.at[u, item], r_wf.at[u, item])
+        for item, rows in enumerate(relays(u, core)):
+            left(wp.at[j, rows], s_ws.at[u, item], r_ws.at[u, item])
+
+    for u in (0, 1, 3, 4):
+        w1(u).start()
 
     block_rows = lax.broadcasted_iota(jnp.int32, (CH, CH), 0)
     block_cols = lax.broadcasted_iota(jnp.int32, (CH, CH), 1)
@@ -217,7 +233,7 @@
             state_step(f, b)
             return carry
 
-        lax.fori_loop(0, blocks, step_of, 0)
+        lax.fori_loop(0, blocks, step_of, 0, unroll=8)
         state[f] = state_f[f].astype(BF16)
         for step in range(1, 2 * NX):
             i = (me + step) % (2 * NX)
@@ -246,8 +262,11 @@
         return carry
 
     loads[3].wait()
-    lax.fori_loop(0, blocks // 2, block_step, 0)
-
+    first_part = 3
+    lax.fori_loop(0, first_part, block_step, 0, unroll=first_part)
+
+
+    stage_a(0)
 
     for f in range(halves):
         for step in range(1, 2 * NX):
@@ -272,8 +291,12 @@
                 rdma(a_out.at[f], a_in.at[f, n], s_a2.at[f, n], r_a2.at[f, n], to, y).start()
                 rdma(t_out.at[f], t_in.at[f, n], s_p2.at[f, n], r_p2.at[f, n], to, y).start()
 
-    stage_a(1)
-    lax.fori_loop(blocks // 2, blocks, block_step, 0)
+        if f == 0:
+            stage_a(1)
+            w1(2).start()
+
+    lax.fori_loop(first_part, blocks, block_step, 0, unroll=blocks - first_part)
+    stage_b(0)
 
     for f in range(halves):
         plane[...] = jnp.zeros_like(plane)
@@ -295,15 +318,20 @@
             ).start()
         e_in[f, rows_of(me), :] = p3[f, me]
 
+    stage_b(1)
     loads[4].wait()
-    stage_b(1)
+    stage_c(0)
 
     for f in range(halves):
         for step in range(1, 2 * NX):
             i = (me + step) % (2 * NX)
             arrived(e_in.at[f, rows_of(i), :], s_p3.at[f, i], r_p3.at[f, i])
 
-    def hidden_step(c, carry):
+    straight = chunks - CROSS
+
+    def hidden_step(step, carry):
+        c = jnp.where(step < 2 * CROSS, step // 2 + (step % 2) * straight, step - CROSS)
+        to = jnp.where(c < straight, pair, over)
         rows = rows_at(c, PIECE)
         for h in range(heads):
             kc = head_keys(h)
@@ -314,15 +342,16 @@
             val = gate[rows, vc].astype(F32)
             silu = val / (1.0 + jnp.exp(-val))
             hid[rows, vc] = (full * lax.rsqrt(mean + 1e-5) * silu).astype(BF16)
-        rdma(hid.at[rows, :], hid_peer.at[rows, :], s_hid.at[c], r_hid.at[c], ctx, pair).start()
+        rdma(hid.at[rows, :], hid_peer.at[rows, :], s_hid.at[c], r_hid.at[c], ctx, to).start()
         return carry
 
     lax.fori_loop(0, chunks, hidden_step, 0)
 
     stage_c(1)
-    stage_a(0)
+    stage_a(2)
     for load in loads[5:]:
         load.wait()
+    stage_d(0)
     stage_d(1)
 
     tile = 512
@@ -334,58 +363,71 @@
 
         lax.fori_loop(0, width // tile, column, 0)
 
-    lag = 8
-    pieces = CH // PIECE
-
-    def main_step(c, carry):
-        @pl.when(c < chunks)
-        def _():
-            rows = rows_at(c, PIECE)
-
-            def own_part(cols):
-                ahead_of[:, cols] = dot(hid[rows, :], wo[1, :, cols], ((1,), (0,)))
-
-            def pair_part(cols):
-                total = ahead_of[:, cols] + dot(hid_peer[rows, :], wp[1, :, cols], ((1,), (0,)))
-                send[rows, cols] = total.astype(BF16)
-
-            columns(own_part)
-            arrived(hid_peer.at[rows, :], s_hid.at[c], r_hid.at[c])
-            columns(pair_part)
-            rdma(send.at[rows, :], recv.at[rows, :], s_rs.at[c], r_rs.at[c], ctx, over).start()
-
-        @pl.when(c == 3)
-        def _():
-            stage_b(0)
-
-        @pl.when(c == 5)
-        def _():
-            stage_c(0)
-
-        @pl.when(c == lag)
-        def _():
-            stage_d(0)
-
-        @pl.when(c >= lag)
-        def _():
-            d = c - lag
-            rows = rows_at(d, CH)
-
-            def both_parts(cols):
-                total = dot(hid[rows, :], wo[0, :, cols], ((1,), (0,)))
-                own[:, cols] = total + dot(hid_peer[rows, :], wp[0, :, cols], ((1,), (0,)))
-
-            columns(both_parts)
-            for piece in range(pieces):
-                got = rows_at(d * pieces + piece, PIECE)
-                n = d * pieces + piece
-                arrived(recv.at[got, :], s_rs.at[n], r_rs.at[n])
-            res[rows, :] = (own[...] + recv[rows, :].astype(F32)).astype(BF16)
-            pltpu.make_async_copy(res.at[rows, :], out_h.at[rows, :], s_out.at[d]).start()
-
+    def own_sums(first, count, j):
+        rows = pl.ds(first * PIECE, count * PIECE)
+
+        def both_parts(cols):
+            total = dot(hid[rows, :], wo[0, :, cols], ((1,), (0,)))
+            own[rows, cols] = total + dot(hid_peer[rows, :], wp[j, :, cols], ((1,), (0,)))
+
+        columns(both_parts)
+
+    def piece_at(step):
+        late = step - (chunks - 2 * CROSS + 1)
+        crossed = jnp.logical_and(late >= 0, late % 2 == 0)
+        behind_cross = step - (late + 1) // 2
+        return jnp.where(late < 0, step, jnp.where(crossed, straight + late // 2, behind_cross))
+
+    def main_step(step, carry):
+        c = piece_at(step)
+        crossed = c >= straight
+        to = jnp.where(crossed, pair, over)
+        jo = jnp.where(crossed, 2, 1)
+        jp = jnp.where(crossed, 3, 1)
+        rows = rows_at(c, PIECE)
+
+        def own_part(cols):
+            ahead_of[:, cols] = dot(hid[rows, :], wo[jo, :, cols], ((1,), (0,)))
+
+        def pair_part(cols):
+            total = ahead_of[:, cols] + dot(hid_peer[rows, :], wp[jp, :, cols], ((1,), (0,)))
+            send[rows, cols] = total.astype(BF16)
+
+        columns(own_part)
+        arrived(hid_peer.at[rows, :], s_hid.at[c], r_hid.at[c])
+        columns(pair_part)
+        rdma(send.at[rows, :], recv.at[rows, :], s_rs.at[c], r_rs.at[c], ctx, to).start()
+
+        def at(when, *actions):
+            @pl.when(step == when)
+            def _():
+                for action, *args in actions:
+                    action(*args)
+
+        at(3, (stage_b, 2), (stage_a, 3))
+        at(5, (stage_c, 2))
+        at(6, (stage_b, 3), (stage_a, 4))
+        at(7, (stage_d, 2), (own_sums, 0, 4, 0))
+        at(8, (stage_c, 3))
+        at(9, (stage_b, 4), (own_sums, 4, 4, 0))
+        at(10, (stage_d, 3))
+        at(11, (stage_c, 4), (own_sums, 8, 4, 0))
         return carry
 
-    lax.fori_loop(0, lag + blocks, main_step, 0)
+    lax.fori_loop(0, chunks, main_step, 0)
+    stage_d(4)
+    own_sums(12, straight - 12, 0)
+    own_sums(straight, CROSS, 2)
+
+    def result_step(step, carry):
+        c = piece_at(step)
+        rows = rows_at(c, PIECE)
+        arrived(recv.at[rows, :], s_rs.at[c], r_rs.at[c])
+        res[rows, :] = (own[rows, :] + recv[rows, :].astype(F32)).astype(BF16)
+        pltpu.make_async_copy(res.at[rows, :], out_h.at[rows, :], s_out.at[c]).start()
+        return carry
+
+    lax.fori_loop(0, chunks, result_step, 0)
 
     for f in range(halves):
         for step in range(1, 2 * NX):
@@ -401,19 +443,37 @@
                 left(a_out.at[f], s_a2.at[f, n], r_a2.at[f, n])
                 left(t_out.at[f], s_p2.at[f, n], r_p2.at[f, n])
 
-    weights_left(1)
-    weights_left(0)
+    for u in range(len(units)):
+        weights_left(u)
 
     def finish(c, carry):
         rows = rows_at(c, PIECE)
         left(hid.at[rows, :], s_hid.at[c], r_hid.at[c])
         left(send.at[rows, :], s_rs.at[c], r_rs.at[c])
+        pltpu.make_async_copy(res.at[rows, :], out_h.at[rows, :], s_out.at[c]).wait()
         return carry
 
     lax.fori_loop(0, chunks, finish, 0)
-    for d in range(blocks):
-        rows = rows_at(d, CH)
-        pltpu.make_async_copy(res.at[rows, :], out_h.at[rows, :], s_out.at[d]).wait()
+
+
+def copy_kernel(src, dst, held, s_in, s_out):
+    parts = s_in.shape[0]
+    size = src.shape[0] // parts
+    reads = [
+        pltpu.make_async_copy(src.at[pl.ds(i * size, size)], held.at[pl.ds(i * size, size)], s_in.at[i])
+        for i in range(parts)
+    ]
+    writes = [
+        pltpu.make_async_copy(held.at[pl.ds(i * size, size)], dst.at[pl.ds(i * size, size)], s_out.at[i])
+        for i in range(parts)
+    ]
+    for read in reads:
+        read.start()
+    for read, write in zip(reads, writes, strict=True):
+        read.wait()
+        write.start()
+    for write in writes:
+        write.wait()
 
 
 def shards(queries, keys, values, log_gate, out_gate, segment_ids, final_projector):
@@ -431,7 +491,7 @@
 
     vm = pltpu.VMEM
     dma = pltpu.SemaphoreType.DMA
-    return pl.pallas_call(
+    projected = pl.pallas_call(
         layer_kernel,
         in_specs=[pl.BlockSpec(memory_space=pltpu.SMEM)] + [pl.BlockSpec(memory_space=pl.ANY)] * 6,
         out_specs=pl.BlockSpec(memory_space=pl.ANY),
@@ -450,14 +510,14 @@
             vm((tokens, vals_wide), BF16),
             vm((tokens, keys_wide), BF16),
             vm((tokens, vals_wide), BF16),
-            vm((2, depth, width), BF16),
-            vm((2, depth, width), BF16),
+            vm((3, depth, width), BF16),
+            vm((4, depth, width), BF16),
             vm((tokens, vals_wide), BF16),
             vm((tokens, vals_wide), BF16),
             vm((tokens, width), BF16),
             vm((tokens, width), BF16),
             vm((tokens, width), BF16),
-            vm((CH, width), F32),
+            vm((tokens, width), F32),
             vm((PIECE, width), F32),
             vm((halves, slots, part, wide), BF16),
             vm((halves, slots, 1, wide), F32),
@@ -475,19 +535,27 @@
             dma((halves, REACH)), dma((halves, REACH)),
             dma((halves, REACH)), dma((halves, REACH)),
             dma((halves, slots)), dma((halves, slots)),
-            dma((2,)), dma((2,)),
-            dma((2, 2)), dma((2, 2)),
-            dma((2, 2)), dma((2, 2)),
-            dma((2, 5)), dma((2, 5)),
+            dma((5,)), dma((5,)),
+            dma((5, 2)), dma((5, 2)),
+            dma((5, 2)), dma((5, 2)),
+            dma((5, 5)), dma((5, 5)),
             dma((chunks,)), dma((chunks,)),
             dma((chunks,)), dma((chunks,)),
-            dma((7,)),
-            dma((blocks,)),
+            dma((8,)),
+            dma((chunks,)),
         ],
         compiler_params=pltpu.CompilerParams(
-            collective_id=0, has_side_effects=True, vmem_limit_bytes=56 * 2**20
+            collective_id=0, has_side_effects=True, vmem_limit_bytes=58 * 2**20
         ),
     )(segment_ids, log_gate, keys, values, queries, out_gate, final_projector)
+    return pl.pallas_call(
+        copy_kernel,
+        in_specs=[pl.BlockSpec(memory_space=pl.ANY)],
+        out_specs=pl.BlockSpec(memory_space=pl.ANY),
+        out_shape=jax.ShapeDtypeStruct((tokens, width), BF16),
+        scratch_shapes=[vm((tokens, width), BF16), dma((4,)), dma((4,))],
+        compiler_params=pltpu.CompilerParams(vmem_limit_bytes=60 * 2**20),
+    )(projected)
 
 
 def solution(mesh):

time: 92.9 us -> 84.6 us (0.911)
  Pallas kernels: 89.7 us -> 84.5 us
  local copies, waits for them, and re-layouts: 3.08 us -> 0 us
    pallas_call x1, Pallas kernels: 89.7 us -> 82 us  [shards(): pl.pallas_call(layer_kernel, in_specs=[pl.BlockSpec(memory_space=pltpu.SM...]
    unnamed x1 -> x0, local copies, waits for them, and re-layouts: 3.08 us -> none
    pallas_call x0 -> x1, Pallas kernels: none -> 2.42 us  [shards(): pl.pallas_call(copy_kernel, in_specs=[pl.BlockSpec(memory_space=pl.ANY)],...]
where the time goes in v4:
time: 84.6 us; the launch traced here: 84.5 us
  Pallas kernels  84.5 us (100%)
    pallas_call x1, Pallas kernels, shards(): pl.pallas_call(layer_kernel, in_specs=[pl.BlockSpec(memory_space=pltpu.SM...  82 us
    pallas_call x1, Pallas kernels, shards(): pl.pallas_call(copy_kernel, in_specs=[pl.BlockSpec(memory_space=pl.ANY)],...  2.42 us

profile of v4, /device:TPU:1, one launch (start us, length us, event | category | flops | bytes accessed | tf_op | source)
XLA Modules:
  0.0 84.5 jit_solution(13052512022795799779)
XLA Ops:
  0.0 82.0 %shard_map.73.src = bf16[1024,1024]{1,0:T(8,128)(2,1)} custom-call(s32[512]{0:T(512)} %seg.1, bf16[1024,512]{1,0:T(8,128)(2,1)} %g_h.1, bf16[1024,512]{1,0:T(8,128)(2,1)} %k_h.1, bf16[1024,1024]{1,0:T(8,128)(2,1)} %v_h.1, bf16[1024,512]{1,0:T(8,128)(2,1)} %q_h.1, bf16[1024,1024]{1,0:T(8,128)(2,1)} %gate_h.1, bf16[1024,4096]{1,0:T(8,128)(2,1)} %proj_h.1), custom_call_target="tpu_custom_call" | custom-call | tf_op jit(solution)/shard_map/pallas_call | solution.py:494
  82.1 2.4 %shard_map.74 = bf16[1024,1024]{1,0:T(8,128)(2,1)} custom-call(bf16[1024,1024]{1,0:T(8,128)(2,1)} %shard_map.73.src), custom_call_target="tpu_custom_call" | custom-call | tf_op jit(solution)/shard_map/pallas_call | solution.py:551

commit v5 on v4

--- a/solution.py
+++ b/solution.py
@@ -79,7 +79,7 @@
             )
         )
     ]
-    for load in loads:
+    for load in loads[:3]:
         load.start()
 
     barrier = pltpu.get_barrier_semaphore()
@@ -202,6 +202,8 @@
 
     for load in loads[:3]:
         load.wait()
+    for load in loads[3:]:
+        load.start()
 
     def state_step(f, b):
         lanes = slice(f * wide, (f + 1) * wide)
@@ -266,8 +268,6 @@
     lax.fori_loop(0, first_part, block_step, 0, unroll=first_part)
 
 
-    stage_a(0)
-
     for f in range(halves):
         for step in range(1, 2 * NX):
             i = (me + step) % (2 * NX)
@@ -291,12 +291,10 @@
                 rdma(a_out.at[f], a_in.at[f, n], s_a2.at[f, n], r_a2.at[f, n], to, y).start()
                 rdma(t_out.at[f], t_in.at[f, n], s_p2.at[f, n], r_p2.at[f, n], to, y).start()
 
-        if f == 0:
-            stage_a(1)
-            w1(2).start()
-
+        stage_a(f)
+
+    w1(2).start()
     lax.fori_loop(first_part, blocks, block_step, 0, unroll=blocks - first_part)
-    stage_b(0)
 
     for f in range(halves):
         plane[...] = jnp.zeros_like(plane)
@@ -318,9 +316,9 @@
             ).start()
         e_in[f, rows_of(me), :] = p3[f, me]
 
+    stage_b(0)
     stage_b(1)
     loads[4].wait()
-    stage_c(0)
 
     for f in range(halves):
         for step in range(1, 2 * NX):
@@ -345,7 +343,9 @@
         rdma(hid.at[rows, :], hid_peer.at[rows, :], s_hid.at[c], r_hid.at[c], ctx, to).start()
         return carry
 
-    lax.fori_loop(0, chunks, hidden_step, 0)
+    lax.fori_loop(0, 2 * CROSS, hidden_step, 0)
+    stage_c(0)
+    lax.fori_loop(2 * CROSS, chunks, hidden_step, 0)
 
     stage_c(1)
     stage_a(2)
@@ -419,16 +419,6 @@
     own_sums(12, straight - 12, 0)
     own_sums(straight, CROSS, 2)
 
-    def result_step(step, carry):
-        c = piece_at(step)
-        rows = rows_at(c, PIECE)
-        arrived(recv.at[rows, :], s_rs.at[c], r_rs.at[c])
-        res[rows, :] = (own[rows, :] + recv[rows, :].astype(F32)).astype(BF16)
-        pltpu.make_async_copy(res.at[rows, :], out_h.at[rows, :], s_out.at[c]).start()
-        return carry
-
-    lax.fori_loop(0, chunks, result_step, 0)
-
     for f in range(halves):
         for step in range(1, 2 * NX):
             i = (me + step) % (2 * NX)
@@ -446,14 +436,36 @@
     for u in range(len(units)):
         weights_left(u)
 
-    def finish(c, carry):
+    def hidden_left(c, carry):
         rows = rows_at(c, PIECE)
         left(hid.at[rows, :], s_hid.at[c], r_hid.at[c])
-        left(send.at[rows, :], s_rs.at[c], r_rs.at[c])
-        pltpu.make_async_copy(res.at[rows, :], out_h.at[rows, :], s_out.at[c]).wait()
         return carry
 
-    lax.fori_loop(0, chunks, finish, 0)
+    lax.fori_loop(0, chunks, hidden_left, 0)
+
+    def store(c):
+        rows = rows_at(c, PIECE)
+        return pltpu.make_async_copy(res.at[rows, :], out_h.at[rows, :], s_out.at[c])
+
+    def result_step(step, carry):
+        c = piece_at(step)
+        rows = rows_at(c, PIECE)
+        arrived(recv.at[rows, :], s_rs.at[c], r_rs.at[c])
+        res[rows, :] = (own[rows, :] + recv[rows, :].astype(F32)).astype(BF16)
+        store(c).start()
+
+        @pl.when(step >= 2)
+        def _():
+            before = piece_at(step - 2)
+            store(before).wait()
+            left(send.at[rows_at(before, PIECE), :], s_rs.at[before], r_rs.at[before])
+
+        return carry
+
+    lax.fori_loop(0, chunks, result_step, 0)
+    for step in range(chunks - 2, chunks):
+        store(piece_at(step)).wait()
+        left(send.at[rows_at(piece_at(step), PIECE), :], s_rs.at[piece_at(step)], r_rs.at[piece_at(step)])
 
 
 def copy_kernel(src, dst, held, s_in, s_out):

time: 84.6 us -> 83.3 us (0.985)
  Pallas kernels: 84.5 us -> 82.8 us
    pallas_call x1, Pallas kernels: 82 us -> 80.4 us  [shards(): pl.pallas_call(layer_kernel, in_specs=[pl.BlockSpec(memory_space=pltpu.SM...]
where the time goes in v5:
time: 83.3 us; the launch traced here: 82.8 us
  Pallas kernels  82.8 us (99%)
    pallas_call x1, Pallas kernels, shards(): pl.pallas_call(layer_kernel, in_specs=[pl.BlockSpec(memory_space=pltpu.SM...  80.4 us
    pallas_call x1, Pallas kernels, shards(): pl.pallas_call(copy_kernel, in_specs=[pl.BlockSpec(memory_space=pl.ANY)],...  2.42 us

profile of v5, /device:TPU:1, one launch (start us, length us, event | category | flops | bytes accessed | tf_op | source)
XLA Modules:
  0.0 82.8 jit_solution(9942041549996464695)
XLA Ops:
  0.0 80.4 %shard_map.73.src = bf16[1024,1024]{1,0:T(8,128)(2,1)} custom-call(s32[512]{0:T(512)} %seg.1, bf16[1024,512]{1,0:T(8,128)(2,1)} %g_h.1, bf16[1024,512]{1,0:T(8,128)(2,1)} %k_h.1, bf16[1024,1024]{1,0:T(8,128)(2,1)} %v_h.1, bf16[1024,512]{1,0:T(8,128)(2,1)} %q_h.1, bf16[1024,1024]{1,0:T(8,128)(2,1)} %gate_h.1, bf16[1024,4096]{1,0:T(8,128)(2,1)} %proj_h.1), custom_call_target="tpu_custom_call" | custom-call | tf_op jit(solution)/shard_map/pallas_call | solution.py:506
  80.4 2.4 %shard_map.74 = bf16[1024,1024]{1,0:T(8,128)(2,1)} custom-call(bf16[1024,1024]{1,0:T(8,128)(2,1)} %shard_map.73.src), custom_call_target="tpu_custom_call" | custom-call | tf_op jit(solution)/shard_map/pallas_call | solution.py:563

commit v6 on v5

--- a/solution.py
+++ b/solution.py
@@ -24,13 +24,13 @@
 
 
 def layer_kernel(
-    seg, g_h, k_h, v_h, q_h, gate_h, proj_h, out_h,
-    g, k, v, q, cum, state_f, state, starts, weights, decay,
-    mixed, reach, gate, wo, wp, hid, hid_peer, send, recv, res, own, ahead_of,
+    seg, g_h, k_h, v_h, q_h, gate_h, proj_h, out,
+    g, k, v, q, cum, state_f, state, starts, weights, decay, weight_now,
+    mixed, reach, gate, wo, wp, hid, hid_peer, send, recv, own, ahead_of,
     p1, a1, xs, acc, t_out, a_out, t_in, a_in, plane, p3, e_in,
     s_p1, r_p1, s_a1, r_a1, s_p2, r_p2, s_a2, r_a2, s_p3, r_p3,
     s_w1, r_w1, s_wx, r_wx, s_wf, r_wf, s_ws, r_ws,
-    s_hid, r_hid, s_rs, r_rs, s_load, s_out,
+    s_hid, r_hid, s_rs, r_rs, s_load,
 ):
     ctx = lax.axis_index("ctx")
     y = lax.axis_index("head")
@@ -186,7 +186,7 @@
     causal = block_cols <= block_rows
     ones = causal.astype(F32).astype(BF16)
     state_f[...] = jnp.zeros_like(state_f)
-    decay[...] = jnp.ones_like(decay)
+    weight_now[...] = jnp.ones_like(weight_now)
     wide = p1.shape[3]
     halves = p1.shape[0]
     group = heads // halves
@@ -205,20 +205,23 @@
     for load in loads[3:]:
         load.start()
 
+    def same_stream(b):
+        at = ctx * blocks + b
+        same = jnp.logical_and(seg[at] == seg[jnp.maximum(at - 1, 0)], at > 0)
+        return jnp.where(same, 1.0, 0.0)
+
     def state_step(f, b):
         lanes = slice(f * wide, (f + 1) * wide)
         rows = rows_at(b, CH)
-        at = ctx * blocks + b
-        same = jnp.logical_and(seg[at] == seg[jnp.maximum(at - 1, 0)], at > 0)
-        keep = jnp.where(same, 1.0, 0.0)
+        keep = same_stream(b)
         sums = dot(ones, g[rows, lanes], ((1,), (0,)))
         cum[rows, lanes] = sums
         last = sums[CH - 1 : CH, :]
         kept = (k[rows, lanes].astype(F32) * jnp.exp(last - sums)).astype(BF16)
         fall = jnp.exp(last)
-        weight = decay[f] * keep
+        weight = weight_now[f] * keep
         weights[b, :, lanes] = weight
-        decay[f] = weight * fall
+        weight_now[f] = weight * fall
         for i in range(group):
             kc = head_keys(i)
             start = state_f[f, :, kc] * keep
@@ -229,6 +232,17 @@
     def rows_of(i):
         return pl.ds(pl.multiple_of(i * part, part), part)
 
+    flags = [same_stream(b) for b in range(blocks)]
+    through = flags[0]
+    for flag in flags[1:]:
+        through = through * flag
+    total = dot(jnp.ones((16, tokens), BF16), g[...], ((1,), (0,)))[:1]
+    decay[...] = jnp.exp(total) * through
+    for step in range(1, 2 * NX):
+        i = (me + step) % (2 * NX)
+        rdma(decay, a1.at[me], s_a1.at[i], r_a1.at[me], base + i, y).start()
+    a1[me] = decay[...]
+
     for f in range(halves):
 
         def step_of(b, carry):
@@ -239,12 +253,10 @@
         state[f] = state_f[f].astype(BF16)
         for step in range(1, 2 * NX):
             i = (me + step) % (2 * NX)
-            rdma(decay.at[f], a1.at[f, me], s_a1.at[f, i], r_a1.at[f, me], base + i, y).start()
             rdma(
                 state.at[f, rows_of(i), :], p1.at[f, me], s_p1.at[f, i], r_p1.at[f, me], base + i, y
             ).start()
         p1[f, me] = state[f, rows_of(me), :]
-        a1[f, me] = decay[f]
 
     def block_step(b, carry):
         rows = rows_at(b, CH)
@@ -268,27 +280,37 @@
     lax.fori_loop(0, first_part, block_step, 0, unroll=first_part)
 
 
+    for step in range(1, 2 * NX):
+        i = (me + step) % (2 * NX)
+        arrived(a1.at[i], s_a1.at[i], r_a1.at[i])
+    scale = jnp.ones_like(decay[...])
+    for i in range(2 * NX):
+        acc[i] = scale
+        scale = scale * a1[i]
+    a_out[...] = scale
+    for far in range(1, REACH + 1):
+
+        @pl.when(z + far < NZ)
+        def _():
+            n = far - 1
+            rdma(a_out, a_in.at[n], s_a2.at[n], r_a2.at[n], ctx + far * 2 * NX, y).start()
+
     for f in range(halves):
         for step in range(1, 2 * NX):
             i = (me + step) % (2 * NX)
-            arrived(a1.at[f, i], s_a1.at[f, i], r_a1.at[f, i])
             arrived(p1.at[f, i], s_p1.at[f, i], r_p1.at[f, i])
         run = jnp.zeros((part, wide), F32)
-        scale = jnp.ones((1, wide), F32)
+        lanes = slice(f * wide, (f + 1) * wide)
         for i in range(2 * NX):
             xs[f, i] = run
-            acc[f, i] = scale
-            run = run * a1[f, i] + p1[f, i].astype(F32)
-            scale = scale * a1[f, i]
+            run = run * a1[i, :, lanes] + p1[f, i].astype(F32)
         t_out[f] = run.astype(BF16)
-        a_out[f] = scale
         for far in range(1, REACH + 1):
 
             @pl.when(z + far < NZ)
             def _():
                 to = ctx + far * 2 * NX
                 n = far - 1
-                rdma(a_out.at[f], a_in.at[f, n], s_a2.at[f, n], r_a2.at[f, n], to, y).start()
                 rdma(t_out.at[f], t_in.at[f, n], s_p2.at[f, n], r_p2.at[f, n], to, y).start()
 
         stage_a(f)
@@ -297,18 +319,20 @@
     lax.fori_loop(first_part, blocks, block_step, 0, unroll=blocks - first_part)
 
     for f in range(halves):
+        lanes = slice(f * wide, (f + 1) * wide)
         plane[...] = jnp.zeros_like(plane)
         for far in range(REACH, 0, -1):
 
             @pl.when(z - far >= 0)
             def _():
                 n = far - 1
-                arrived(a_in.at[f, n], s_a2.at[f, n], r_a2.at[f, n])
+                if f == 0:
+                    arrived(a_in.at[n], s_a2.at[n], r_a2.at[n])
                 arrived(t_in.at[f, n], s_p2.at[f, n], r_p2.at[f, n])
-                plane[...] = plane[...] * a_in[f, n] + t_in[f, n].astype(F32)
+                plane[...] = plane[...] * a_in[n, :, lanes] + t_in[f, n].astype(F32)
 
         for i in range(2 * NX):
-            p3[f, i] = (xs[f, i] + acc[f, i] * plane[...]).astype(BF16)
+            p3[f, i] = (xs[f, i] + acc[i, :, lanes] * plane[...]).astype(BF16)
         for step in range(1, 2 * NX):
             i = (me + step) % (2 * NX)
             rdma(
@@ -409,9 +433,10 @@
         at(6, (stage_b, 3), (stage_a, 4))
         at(7, (stage_d, 2), (own_sums, 0, 4, 0))
         at(8, (stage_c, 3))
-        at(9, (stage_b, 4), (own_sums, 4, 4, 0))
+        at(9, (own_sums, 4, 4, 0))
         at(10, (stage_d, 3))
-        at(11, (stage_c, 4), (own_sums, 8, 4, 0))
+        at(11, (stage_b, 4), (own_sums, 8, 4, 0))
+        at(14, (stage_c, 4))
         return carry
 
     lax.fori_loop(0, chunks, main_step, 0)
@@ -422,7 +447,8 @@
     for f in range(halves):
         for step in range(1, 2 * NX):
             i = (me + step) % (2 * NX)
-            left(decay.at[f], s_a1.at[f, i], r_a1.at[f, i])
+            if f == 0:
+                left(decay, s_a1.at[i], r_a1.at[i])
             left(p1.at[f, i], s_p1.at[f, i], r_p1.at[f, i])
             left(p3.at[f, i], s_p3.at[f, i], r_p3.at[f, i])
         for far in range(1, REACH + 1):
@@ -430,7 +456,8 @@
             @pl.when(z + far < NZ)
             def _():
                 n = far - 1
-                left(a_out.at[f], s_a2.at[f, n], r_a2.at[f, n])
+                if f == 0:
+                    left(a_out, s_a2.at[n], r_a2.at[n])
                 left(t_out.at[f], s_p2.at[f, n], r_p2.at[f, n])
 
     for u in range(len(units)):
@@ -443,46 +470,32 @@
 
     lax.fori_loop(0, chunks, hidden_left, 0)
 
-    def store(c):
-        rows = rows_at(c, PIECE)
-        return pltpu.make_async_copy(res.at[rows, :], out_h.at[rows, :], s_out.at[c])
-
     def result_step(step, carry):
         c = piece_at(step)
         rows = rows_at(c, PIECE)
         arrived(recv.at[rows, :], s_rs.at[c], r_rs.at[c])
-        res[rows, :] = (own[rows, :] + recv[rows, :].astype(F32)).astype(BF16)
-        store(c).start()
+        out[rows, :] = (own[rows, :] + recv[rows, :].astype(F32)).astype(BF16)
 
         @pl.when(step >= 2)
         def _():
             before = piece_at(step - 2)
-            store(before).wait()
             left(send.at[rows_at(before, PIECE), :], s_rs.at[before], r_rs.at[before])
 
         return carry
 
     lax.fori_loop(0, chunks, result_step, 0)
     for step in range(chunks - 2, chunks):
-        store(piece_at(step)).wait()
         left(send.at[rows_at(piece_at(step), PIECE), :], s_rs.at[piece_at(step)], r_rs.at[piece_at(step)])
 
 
-def copy_kernel(src, dst, held, s_in, s_out):
-    parts = s_in.shape[0]
+def copy_kernel(src, dst, sems):
+    parts = sems.shape[0]
     size = src.shape[0] // parts
-    reads = [
-        pltpu.make_async_copy(src.at[pl.ds(i * size, size)], held.at[pl.ds(i * size, size)], s_in.at[i])
+    writes = [
+        pltpu.make_async_copy(src.at[pl.ds(i * size, size)], dst.at[pl.ds(i * size, size)], sems.at[i])
         for i in range(parts)
     ]
-    writes = [
-        pltpu.make_async_copy(held.at[pl.ds(i * size, size)], dst.at[pl.ds(i * size, size)], s_out.at[i])
-        for i in range(parts)
-    ]
-    for read in reads:
-        read.start()
-    for read, write in zip(reads, writes, strict=True):
-        read.wait()
+    for write in writes:
         write.start()
     for write in writes:
         write.wait()
@@ -506,8 +519,8 @@
     projected = pl.pallas_call(
         layer_kernel,
         in_specs=[pl.BlockSpec(memory_space=pltpu.SMEM)] + [pl.BlockSpec(memory_space=pl.ANY)] * 6,
-        out_specs=pl.BlockSpec(memory_space=pl.ANY),
-        out_shape=jax.ShapeDtypeStruct((tokens, width), BF16),
+        out_specs=pl.BlockSpec(memory_space=pltpu.VMEM),
+        out_shape=pltpu.VMEM((tokens, width), BF16),
         scratch_shapes=[
             vm((tokens, keys_wide), BF16),
             vm((tokens, keys_wide), BF16),
@@ -518,6 +531,7 @@
             vm((halves, DV, wide), BF16),
             vm((blocks, DV, keys_wide), BF16),
             vm((blocks, 1, keys_wide), F32),
+            vm((1, keys_wide), F32),
             vm((halves, 1, wide), F32),
             vm((tokens, vals_wide), BF16),
             vm((tokens, keys_wide), BF16),
@@ -528,24 +542,23 @@
             vm((tokens, vals_wide), BF16),
             vm((tokens, width), BF16),
             vm((tokens, width), BF16),
-            vm((tokens, width), BF16),
             vm((tokens, width), F32),
             vm((PIECE, width), F32),
             vm((halves, slots, part, wide), BF16),
-            vm((halves, slots, 1, wide), F32),
+            vm((slots, 1, keys_wide), F32),
             vm((halves, slots, part, wide), F32),
-            vm((halves, slots, 1, wide), F32),
+            vm((slots, 1, keys_wide), F32),
             vm((halves, part, wide), BF16),
-            vm((halves, 1, wide), F32),
+            vm((1, keys_wide), F32),
             vm((halves, REACH, part, wide), BF16),
-            vm((halves, REACH, 1, wide), F32),
+            vm((REACH, 1, keys_wide), F32),
             vm((part, wide), F32),
             vm((halves, slots, part, wide), BF16),
             vm((halves, DV, wide), BF16),
             dma((halves, slots)), dma((halves, slots)),
-            dma((halves, slots)), dma((halves, slots)),
+            dma((slots,)), dma((slots,)),
             dma((halves, REACH)), dma((halves, REACH)),
-            dma((halves, REACH)), dma((halves, REACH)),
+            dma((REACH,)), dma((REACH,)),
             dma((halves, slots)), dma((halves, slots)),
             dma((5,)), dma((5,)),
             dma((5, 2)), dma((5, 2)),
@@ -554,7 +567,6 @@
             dma((chunks,)), dma((chunks,)),
             dma((chunks,)), dma((chunks,)),
             dma((8,)),
-            dma((chunks,)),
         ],
         compiler_params=pltpu.CompilerParams(
             collective_id=0, has_side_effects=True, vmem_limit_bytes=58 * 2**20
@@ -562,11 +574,11 @@
     )(segment_ids, log_gate, keys, values, queries, out_gate, final_projector)
     return pl.pallas_call(
         copy_kernel,
-        in_specs=[pl.BlockSpec(memory_space=pl.ANY)],
+        in_specs=[pl.BlockSpec(memory_space=pltpu.VMEM)],
         out_specs=pl.BlockSpec(memory_space=pl.ANY),
         out_shape=jax.ShapeDtypeStruct((tokens, width), BF16),
-        scratch_shapes=[vm((tokens, width), BF16), dma((4,)), dma((4,))],
-        compiler_params=pltpu.CompilerParams(vmem_limit_bytes=60 * 2**20),
+        scratch_shapes=[dma((4,))],
+        compiler_params=pltpu.CompilerParams(vmem_limit_bytes=16 * 2**20),
     )(projected)
 
 

time: 83.3 us -> 82.2 us (0.987)
    pallas_call x1, Pallas kernels: 2.42 us -> 1.35 us  [shards(): pl.pallas_call(copy_kernel, in_specs=[pl.BlockSpec(memory_space=pltpu.VME...]
where the time goes in v6:
time: 82.2 us; the launch traced here: 82.1 us
  Pallas kernels  82.1 us (100%)
    pallas_call x1, Pallas kernels, shards(): pl.pallas_call(layer_kernel, in_specs=[pl.BlockSpec(memory_space=pltpu.SM...  80.7 us

profile of v6, /device:TPU:1, one launch (start us, length us, event | category | flops | bytes accessed | tf_op | source)
XLA Modules:
  0.0 82.1 jit_solution(16827090271310698670)
XLA Ops:
  0.0 80.7 %shard_map.73.src = bf16[1024,1024]{1,0:T(8,128)(2,1)S(1)} custom-call(s32[512]{0:T(512)} %seg.1, bf16[1024,512]{1,0:T(8,128)(2,1)} %g_h.1, bf16[1024,512]{1,0:T(8,128)(2,1)} %k_h.1, bf16[1024,1024]{1,0:T(8,128)(2,1)} %v_h.1, bf16[1024,512]{1,0:T(8,128)(2,1)} %q_h.1, bf16[1024,1024]{1,0:T(8,128)(2,1)} %gate_h.1, bf16[1024,4096]{1,0:T(8,128)(2,1)} %proj_h.1), custom_call_target="tpu_custom_call" | custom-call | tf_op jit(solution)/shard_map/pallas_call | solution.py:519
  80.7 1.3 %shard_map.74 = bf16[1024,1024]{1,0:T(8,128)(2,1)} custom-call(bf16[1024,1024]{1,0:T(8,128)(2,1)S(1)} %shard_map.73.src), custom_call_target="tpu_custom_call" | custom-call | tf_op jit(solution)/shard_map/pallas_call | solution.py:575

commit v7 on v6

--- a/solution.py
+++ b/solution.py
@@ -13,6 +13,7 @@
 MESH = pl.DeviceIdType.MESH
 
 NX = 4
+FAR_FIRST = (4, 3, 5, 2, 6, 1, 7)
 NZ = 8
 PIECE = 64
 CROSS = 2
@@ -232,17 +233,6 @@
     def rows_of(i):
         return pl.ds(pl.multiple_of(i * part, part), part)
 
-    flags = [same_stream(b) for b in range(blocks)]
-    through = flags[0]
-    for flag in flags[1:]:
-        through = through * flag
-    total = dot(jnp.ones((16, tokens), BF16), g[...], ((1,), (0,)))[:1]
-    decay[...] = jnp.exp(total) * through
-    for step in range(1, 2 * NX):
-        i = (me + step) % (2 * NX)
-        rdma(decay, a1.at[me], s_a1.at[i], r_a1.at[me], base + i, y).start()
-    a1[me] = decay[...]
-
     for f in range(halves):
 
         def step_of(b, carry):
@@ -251,12 +241,24 @@
 
         lax.fori_loop(0, blocks, step_of, 0, unroll=8)
         state[f] = state_f[f].astype(BF16)
-        for step in range(1, 2 * NX):
+        for step in FAR_FIRST:
             i = (me + step) % (2 * NX)
             rdma(
                 state.at[f, rows_of(i), :], p1.at[f, me], s_p1.at[f, i], r_p1.at[f, me], base + i, y
             ).start()
         p1[f, me] = state[f, rows_of(me), :]
+
+        if f == 0:
+            flags = [same_stream(b) for b in range(blocks)]
+            through = flags[0]
+            for flag in flags[1:]:
+                through = through * flag
+            total = dot(jnp.ones((16, tokens), BF16), g[...], ((1,), (0,)))[:1]
+            decay[...] = jnp.exp(total) * through
+            for step in range(1, 2 * NX):
+                i = (me + step) % (2 * NX)
+                rdma(decay, a1.at[me], s_a1.at[i], r_a1.at[me], base + i, y).start()
+            a1[me] = decay[...]
 
     def block_step(b, carry):
         rows = rows_at(b, CH)
@@ -305,7 +307,7 @@
             xs[f, i] = run
             run = run * a1[i, :, lanes] + p1[f, i].astype(F32)
         t_out[f] = run.astype(BF16)
-        for far in range(1, REACH + 1):
+        for far in range(REACH, 0, -1):
 
             @pl.when(z + far < NZ)
             def _():
@@ -333,7 +335,7 @@
 
         for i in range(2 * NX):
             p3[f, i] = (xs[f, i] + acc[i, :, lanes] * plane[...]).astype(BF16)
-        for step in range(1, 2 * NX):
+        for step in FAR_FIRST:
             i = (me + step) % (2 * NX)
             rdma(
                 p3.at[f, i], e_in.at[f, rows_of(me), :], s_p3.at[f, i], r_p3.at[f, me], base + i, y

time: 82.2 us -> 81.8 us (level)
  no operation moved by 1% of the time
where the time goes in v7:
time: 81.8 us; the launch traced here: 81.7 us
  Pallas kernels  81.7 us (100%)
    pallas_call x1, Pallas kernels, shards(): pl.pallas_call(layer_kernel, in_specs=[pl.BlockSpec(memory_space=pltpu.SM...  80.3 us

profile of v7, /device:TPU:1, one launch (start us, length us, event | category | flops | bytes accessed | tf_op | source)
XLA Modules:
  0.0 81.7 jit_solution(15318353970722086923)
XLA Ops:
  0.0 80.3 %shard_map.73.src = bf16[1024,1024]{1,0:T(8,128)(2,1)S(1)} custom-call(s32[512]{0:T(512)} %seg.1, bf16[1024,512]{1,0:T(8,128)(2,1)} %g_h.1, bf16[1024,512]{1,0:T(8,128)(2,1)} %k_h.1, bf16[1024,1024]{1,0:T(8,128)(2,1)} %v_h.1, bf16[1024,512]{1,0:T(8,128)(2,1)} %q_h.1, bf16[1024,1024]{1,0:T(8,128)(2,1)} %gate_h.1, bf16[1024,4096]{1,0:T(8,128)(2,1)} %proj_h.1), custom_call_target="tpu_custom_call" | custom-call | tf_op jit(solution)/shard_map/pallas_call | solution.py:521
  80.3 1.3 %shard_map.74 = bf16[1024,1024]{1,0:T(8,128)(2,1)} custom-call(bf16[1024,1024]{1,0:T(8,128)(2,1)S(1)} %shard_map.73.src), custom_call_target="tpu_custom_call" | custom-call | tf_op jit(solution)/shard_map/pallas_call | solution.py:577

commit v8 on v7

--- a/solution.py
+++ b/solution.py
@@ -387,7 +387,7 @@
             do(pl.ds(pl.multiple_of(n * tile, tile), tile))
             return carry
 
-        lax.fori_loop(0, width // tile, column, 0)
+        lax.fori_loop(0, width // tile, column, 0, unroll=2)
 
     def own_sums(first, count, j):
         rows = pl.ds(first * PIECE, count * PIECE)

time: 81.8 us -> 81.6 us (level)
  no operation moved by 1% of the time
where the time goes in v8:
time: 81.6 us; the launch traced here: 81.4 us
  Pallas kernels  81.4 us (100%)
    pallas_call x1, Pallas kernels, shards(): pl.pallas_call(layer_kernel, in_specs=[pl.BlockSpec(memory_space=pltpu.SM...  80.1 us

profile of v8, /device:TPU:1, one launch (start us, length us, event | category | flops | bytes accessed | tf_op | source)
XLA Modules:
  0.0 81.4 jit_solution(13678196639023899146)
XLA Ops:
  0.0 80.1 %shard_map.73.src = bf16[1024,1024]{1,0:T(8,128)(2,1)S(1)} custom-call(s32[512]{0:T(512)} %seg.1, bf16[1024,512]{1,0:T(8,128)(2,1)} %g_h.1, bf16[1024,512]{1,0:T(8,128)(2,1)} %k_h.1, bf16[1024,1024]{1,0:T(8,128)(2,1)} %v_h.1, bf16[1024,512]{1,0:T(8,128)(2,1)} %q_h.1, bf16[1024,1024]{1,0:T(8,128)(2,1)} %gate_h.1, bf16[1024,4096]{1,0:T(8,128)(2,1)} %proj_h.1), custom_call_target="tpu_custom_call" | custom-call | tf_op jit(solution)/shard_map/pallas_call | solution.py:521
  80.1 1.3 %shard_map.74 = bf16[1024,1024]{1,0:T(8,128)(2,1)} custom-call(bf16[1024,1024]{1,0:T(8,128)(2,1)S(1)} %shard_map.73.src), custom_call_target="tpu_custom_call" | custom-call | tf_op jit(solution)/shard_map/pallas_call | solution.py:577
